TPU v7x, 32 devices: a whole 2x2x4 slice. The times are simulated.
32 devices in a mesh: shard: 2 (over x), heads: 4 (over y, core), tensor: 4 (over z).
Axes of the slice: x: 2, y: 2, z: 4, core: 2. Of those that a mesh axis runs over, the one named last changes fastest.
Arguments:
- tokens: bfloat16 [12608, 768], P(('shard', 'heads', 'tensor')), may hold values from -6 to 6
- ln1_gain: bfloat16 [768], P('shard'), may hold values from 0.5 to 1.5
- ln1_bias: bfloat16 [768], P('shard'), may hold values from -2 to 2
- qkv_weight: bfloat16 [768, 2304], P('shard'), may hold values from -0.21875 to 0.21875
- out_weight: bfloat16 [768, 768], P('shard'), may hold values from -1.75 to 1.75
- ln2_gain: bfloat16 [768], P('shard'), may hold values from 0.5 to 1.5
- ln2_bias: bfloat16 [768], P('shard'), may hold values from -2 to 2
- router_weight: bfloat16 [768, 8], P('shard'), may hold values from -0.109375 to 0.109375
- expert_in: bfloat16 [8, 768, 3072], P(None, 'shard', 'tensor'), may hold values from -0.21875 to 0.21875
- expert_out: bfloat16 [8, 3072, 768], P(None, 'tensor', 'shard'), may hold values from -0.4375 to 0.4375
- route_noise: float32 [12608, 8], P(('shard', 'heads', 'tensor')), may hold values from -3 to 3
- expert_ids: int32 [12608, 2], P(('shard', 'heads', 'tensor')), may hold values from 0 to 7, all different within a row
- cotangent: bfloat16 [12608, 768], P(('shard', 'heads', 'tensor')), may hold values from -6 to 6
Outputs:
- mixed: bfloat16 [12608, 768], P(('shard', 'heads', 'tensor'))
- grad_tokens: bfloat16 [12608, 768], P(('shard', 'heads', 'tensor'))
- grad_ln1_gain: float32 [768], P('shard')
- grad_ln1_bias: float32 [768], P('shard')
- grad_qkv_weight: float32 [768, 2304], P('shard')
- grad_out_weight: float32 [768, 768], P('shard')
- grad_ln2_gain: float32 [768], P('shard')
- grad_ln2_bias: float32 [768], P('shard')
- grad_router_weight: float32 [768, 8], P('shard')
- grad_expert_in: float32 [8, 768, 3072], P(None, 'shard', 'tensor')
- grad_expert_out: float32 [8, 3072, 768], P(None, 'tensor', 'shard')
Inputs may be any that keep to these rules, and one draw needn't show every extreme that they name: `expert_ids`: each row names 2 different experts.
All inputs are finite; a program needn't handle non-finite values.
Results may differ from a plain program's by a relative error of at most 0.02.
Values may be sent and summed in bfloat16 or wider, within the bound.
A program may use at most 320 MiB of HBM per device.

v0:
```python
import jax
import jax.numpy as jnp
from jax import lax
from jax.experimental import pallas as pl
from jax.experimental.pallas import tpu as pltpu
from jax.sharding import PartitionSpec as P

HEAD_DIM = 64
SEQ = 197
EPS = 1e-06
AXES = ("shard", "heads", "tensor")
BF = jnp.bfloat16
F32 = jnp.float32


def contract_rows(left, right):
    return lax.dot_general(left, right, (((0,), (0,)), ((), ())), preferred_element_type=F32)


def contract_cols(left, right):
    return lax.dot_general(left, right, (((1,), (1,)), ((), ())), preferred_element_type=F32)


PAD = 208
TILE = 128
CHUNK = 256
FAR = 512.0
TALL = 16
LANES = 128
MASKED = -1e30
CUBIC = 0.044715
ROOT = (2.0 / 3.141592653589793) ** 0.5
BIG = 60 * 1024 * 1024
MESH = pl.DeviceIdType.MESH


def dot(left, right):
    return jnp.dot(left, right, preferred_element_type=F32)


def norm_parts(values):
    centred = values - jnp.mean(values, -1, keepdims=True)
    inverse = lax.rsqrt(jnp.mean(centred * centred, -1, keepdims=True) + EPS)
    return centred * inverse, inverse


def norm_back(grad, unit, inverse, gain):
    scaled = grad * gain
    along = jnp.mean(scaled * unit, -1, keepdims=True)
    return inverse * (scaled - jnp.mean(scaled, -1, keepdims=True) - unit * along)


def head_probs(query, keys, scale):
    scores = contract_cols(query, keys) * scale
    column = lax.broadcasted_iota(jnp.int32, scores.shape, 1)
    scores = jnp.where(column < SEQ, scores, MASKED)
    raised = jnp.exp(scores - jnp.max(scores, -1, keepdims=True))
    return raised / jnp.sum(raised, -1, keepdims=True)


def gain_row(small_ref, experts, index):
    row = slice(experts + index, experts + index + 1)
    return jnp.concatenate((small_ref[0, row, :], small_ref[1, row, :]), 1).astype(F32)


def router_rows(small_ref):
    return jnp.concatenate((small_ref[0], small_ref[1]), 1)


def attend(normed, at, qkv_ref, packed_ref):
    width = normed.shape[1]
    group = 3 * HEAD_DIM
    scale = HEAD_DIM ** (-0.5)
    lane = lax.broadcasted_iota(jnp.int32, (PAD, group), 1) // HEAD_DIM
    outs = []
    for double in range(width // group // 2):
        cols = pl.ds(double * 6 * group, 6 * group)
        packed = dot(normed, qkv_ref[:, cols])
        packed_ref[at, cols] = packed.astype(BF)
        for side in range(2):
            query, keys, values = (
                packed[:, (3 * side + k) * group : (3 * side + k + 1) * group].astype(BF)
                for k in range(3)
            )
            total = jnp.zeros((PAD, group), F32)
            for head in range(3):
                mask = lane == head
                probs = head_probs(jnp.where(mask, query, jnp.zeros_like(query)), keys, scale)
                total = jnp.where(mask, dot(probs.astype(BF), values), total)
            outs.append(total)
    return jnp.concatenate(outs, 1).astype(BF)


def route(normed, small_ref, noise, ids, experts):
    logits = contract_cols(router_rows(small_ref), normed) + noise
    row = lax.broadcasted_iota(jnp.int32, logits.shape, 0)
    logits = jnp.where(row < experts, logits, MASKED)
    raised = jnp.exp(logits - jnp.max(logits, 0, keepdims=True))
    probs = raised / jnp.sum(raised, 0, keepdims=True)
    chosen = ((row == ids[0:1]) | (row == ids[1:2])).astype(F32)
    shifted = row - experts
    flags = (((shifted == ids[0:1]) | (shifted == ids[1:2])) & (shifted >= 0)).astype(F32)
    return probs, probs * chosen + flags


def front_image(image, experts, x_ref, small_ref, qkv_ref, out_ref, noise_ref, ids_ref, keep, ready=None):
    normed_ref, packed_ref, attended_ref, middle_ref = keep
    at = pl.ds(image * PAD, PAD)
    x = x_ref[at, :].astype(F32)
    unit, _ = norm_parts(x)
    normed = (unit * gain_row(small_ref, experts, 0) + gain_row(small_ref, experts, 1)).astype(BF)
    normed_ref[at, :] = normed
    attended = attend(normed, at, qkv_ref, packed_ref)
    attended_ref[at, :] = attended
    if ready is not None:
        ready()
    middle = x + dot(attended, out_ref[...])
    middle_ref[at, :] = middle
    unit, _ = norm_parts(middle)
    normed = (unit * gain_row(small_ref, experts, 2) + gain_row(small_ref, experts, 3)).astype(BF)
    cols = slice(image * PAD, (image + 1) * PAD)
    probs, flags = route(normed, small_ref, noise_ref[:, cols], ids_ref[:, cols], experts)
    return normed, probs, flags


def front_kernel(
    x_ref, small_ref, qkv_ref, out_ref, noise_ref, ids_ref,
    normed_ref, packed_ref, attended_ref, middle_ref, rows_ref, flag_ref, prob_ref,
):
    keep = (normed_ref, packed_ref, attended_ref, middle_ref)
    probs, flags = [], []
    for image in range(x_ref.shape[0] // PAD):
        normed, prob, flag = front_image(
            image, TALL // 2, x_ref, small_ref, qkv_ref, out_ref, noise_ref, ids_ref, keep
        )
        rows_ref[pl.ds(image * PAD, PAD), :] = normed
        probs.append(prob)
        flags.append(flag)
    prob_ref[...] = jnp.concatenate(probs, 1)
    flag_ref[...] = jnp.concatenate(flags, 1).astype(BF)


def front(x, small, qkv, out, noise, ids):
    rows, width = x.shape
    shape = jax.ShapeDtypeStruct
    return pl.pallas_call(
        front_kernel,
        out_shape=(
            shape((rows, width), BF),
            shape((rows, 3 * width), BF),
            shape((rows, width), BF),
            shape((rows, width), F32),
            shape((rows, width), BF),
            shape((TALL, rows), BF),
            shape((TALL, rows), F32),
        ),
        compiler_params=pltpu.CompilerParams(vmem_limit_bytes=BIG),
        cost_estimate=pl.CostEstimate(flops=8 * 10**9, bytes_accessed=10**7, transcendentals=10**6),
        name="front",
    )(x, small, qkv, out, noise, ids)


class Place:
    def __init__(self):
        shard, head, tensor = (lax.axis_index(axis) for axis in AXES)
        self.shard, self.head, self.tensor = shard, head, tensor
        self.pair, self.side = lax.rem(head, 2), lax.div(head, 2)
        self.across = (1 - shard, head, tensor)
        self.beside = (shard, lax.rem(head + 2, 4), tensor)
        self.twin = (shard, head + 1 - 2 * self.pair, tensor)
        self.above = (shard, head, lax.rem(tensor + 1, 4))
        self.below = (shard, head, lax.rem(tensor + 3, 4))

    def greet(self, line=False):
        barrier = pltpu.get_barrier_semaphore()
        devices = [self.across, self.beside, self.twin, self.above, self.below]
        if line:
            devices.append((self.shard, self.head, lax.rem(self.tensor + 2, 4)))
        for device in devices:
            pl.semaphore_signal(barrier, inc=1, device_id=device, device_id_type=MESH)
        pl.semaphore_wait(barrier, len(devices))


class Links:
    def __init__(self, send, recv):
        self.send, self.recv, self.used = send, recv, 0
        self.sent = []

    def copy(self, source, target, device):
        index = self.used
        self.used += 1
        return pltpu.make_async_remote_copy(
            src_ref=source, dst_ref=target, send_sem=self.send.at[index], recv_sem=self.recv.at[index],
            device_id=device, device_id_type=MESH,
        )

    def start(self, source, target, device):
        copy = self.copy(source, target, device)
        copy.start()
        self.sent.append((None, copy))
        return copy

    def skip(self, done):
        self.sent = [(when, copy) for when, copy in self.sent if copy is not done]

    def finish(self):
        for when, copy in self.sent:
            if when is None:
                copy.wait_send()
            else:
                pl.when(when)(copy.wait_send)


class LineGather:
    def __init__(self, links, place, view, own, parts):
        self.links, self.place, self.view, self.own = links, place, view, own
        self.copies = {}
        self.parts = parts

    def start(self, part, step):
        t = self.place.tensor
        for name, slot, device, sends in (
            ("up", t - step, self.place.above, (t >= step) & (t < 3)),
            ("down", t + step, self.place.below, (t + step <= 3) & (t > 0)),
        ):
            slot = jnp.clip(slot, 0, 3)
            source = self.own(part) if step == 0 else self.view(slot, part)
            copy = self.links.copy(source, self.view(slot, part), device)
            pl.when(sends)(copy.start)
            self.links.sent.append((sends, copy))
            self.copies[name, part, step] = copy

    def wait(self, part, step, then=None):
        t = self.place.tensor
        for name, slot, comes in (("up", t - 1 - step, t >= step + 1), ("down", t + 1 + step, t + 1 + step <= 3)):
            copy = self.copies[name, part, step]

            @pl.when(comes)
            def _():
                copy.wait_recv()

    def arrived(self, step):
        t = self.place.tensor
        return (
            (jnp.clip(t - 1 - step, 0, 3), t >= step + 1),
            (jnp.clip(t + 1 + step, 0, 3), t + 1 + step <= 3),
        )


def head_kernel(
    x_ref, cot_ref, small_own, qkv_own, out_own, expert_in, expert_out, noise_ref, ids_ref,
    small_ref, qkv_ref, out_ref, normed_ref, packed_ref, attended_ref, middle_ref, prob_ref,
    rows_all, flags_all, cot_all, got_in, got_out,
    sent_rows, sent_flags, send, recv, local_sem,
):
    place = Place()
    links = Links(send, recv)
    width = x_ref.shape[1]
    experts = expert_in.shape[0]
    depth = qkv_own.shape[0]
    quarter = depth // 4
    shard, pair, side, tensor = place.shard, place.pair, place.side, place.tensor
    mine = pair * 4 + tensor
    place.greet()

    def dense_rows(owner, across_side, across_pair, start, size):
        return pl.ds(pl.multiple_of(owner * depth + (across_side * 2 + across_pair) * quarter + start, TALL), size)

    pieces = ((qkv_own, qkv_ref, 0, quarter // 2), (qkv_own, qkv_ref, quarter // 2, quarter // 2), (out_own, out_ref, 0, quarter))
    smalls = links.start(small_own, small_ref.at[shard], place.across)
    cross = []
    for own, full, start, size in pieces:
        source = own.at[pl.ds(pl.multiple_of((side * 2 + pair) * quarter + start, TALL), size), :]
        cross.append(links.start(source, full.at[dense_rows(shard, side, pair, start, size), :], place.across))

    def expert_item(item):
        index = side * 2 + item // 2
        source, target = (expert_in, got_in) if item % 2 == 0 else (expert_out, got_out)
        return source.at[pair * (experts // 2) + index], target.at[index]

    fetched = [links.start(*expert_item(item), place.across) for item in range(4)]
    here = pl.ds(pl.multiple_of(shard * depth, TALL), depth)
    locals_ = [
        pltpu.make_async_copy(qkv_own, qkv_ref.at[here, :], local_sem.at[0]),
        pltpu.make_async_copy(out_own, out_ref.at[here, :], local_sem.at[1]),
        pltpu.make_async_copy(small_own, small_ref.at[shard], local_sem.at[2]),
        pltpu.make_async_copy(cot_ref, cot_all.at[mine], local_sem.at[3]),
    ]
    for copy in locals_:
        copy.start()

    def slots(array):
        def view(slot, part):
            return array.at[pair * 4 + slot, pl.ds(part * PAD, PAD), :]

        return view

    cot_line = LineGather(links, place, slots(cot_all), lambda part: cot_ref.at[pl.ds(part * PAD, PAD), :], 2)
    for part in range(2):
        cot_line.start(part, 0)

    beside, twins = [], []
    for index, (own, full, start, size) in enumerate(pieces):
        cross[index].wait_recv()
        rows = full.at[dense_rows(1 - shard, side, pair, start, size), :]
        beside.append(links.start(rows, rows, place.beside))
        twins.append(links.start(rows, rows, place.twin))
    for part in range(2):
        cot_line.wait(part, 0)
        cot_line.start(part, 1)
    for index, (own, full, start, size) in enumerate(pieces):
        beside[index].wait_recv()
        rows = full.at[dense_rows(1 - shard, 1 - side, pair, start, size), :]
        twins.append(links.start(rows, rows, place.twin))

    for part in range(2):
        cot_line.wait(part, 1)
        cot_line.start(part, 2)
    smalls.wait_recv()
    for index, copy in enumerate(twins):
        if index % len(pieces) < 2:
            copy.wait_recv()
    for copy in locals_:
        copy.wait()

    keep = (normed_ref, packed_ref, attended_ref, middle_ref)
    row_line = LineGather(links, place, slots(rows_all), lambda part: sent_rows.at[pl.ds(part * PAD, PAD), :], 2)
    flag_line = LineGather(links, place, lambda slot, part: flags_all.at[pair * 4 + slot], lambda part: sent_flags, 1)
    probs, flags = [], []

    def out_ready():
        for index, copy in enumerate(twins):
            if index % len(pieces) == 2:
                copy.wait_recv()

    twin_rows = []
    forwarded = []

    def forward_expert(item):
        fetched[item].wait_recv()
        _, target = expert_item(item)
        forwarded.append(links.start(target, target, place.beside))

    for image in range(2):
        normed, prob, flag = front_image(
            image, experts, x_ref, small_ref, qkv_ref, out_ref, noise_ref, ids_ref, keep,
            out_ready if image == 0 else None,
        )
        at = pl.ds(image * PAD, PAD)
        sent_rows[at, :] = normed
        row_line.start(image, 0)
        twin_rows.append(links.start(sent_rows.at[at, :], rows_all.at[mine, at, :], place.twin))
        probs.append(prob)
        flags.append(flag)
        forward_expert(image)
    prob_ref[...] = jnp.concatenate(probs, 1)
    sent_flags[...] = jnp.concatenate(flags, 1).astype(BF)
    flag_line.start(0, 0)
    twin_flags = [links.start(sent_flags, flags_all.at[mine], place.twin)]
    keep_own = [
        pltpu.make_async_copy(sent_rows, rows_all.at[mine], local_sem.at[0]),
        pltpu.make_async_copy(sent_flags, flags_all.at[mine], local_sem.at[1]),
    ]
    for copy in keep_own:
        copy.start()

    def share(line, array, part, step, copies, whole):
        for slot, comes in line.arrived(step):
            index = pair * 4 + slot
            ref = array.at[index] if whole else array.at[index, pl.ds(part * PAD, PAD), :]
            copy = links.copy(ref, ref, place.twin)
            pl.when(comes)(copy.start)
            links.sent.append((comes, copy))
            copies.append((comes, copy))

    twin_steps = []
    for step in range(3):
        for part in range(2):
            row_line.wait(part, step)
            if step < 2:
                row_line.start(part, step + 1)
            share(row_line, rows_all, part, step, twin_steps, False)
        if step < 2:
            forward_expert(step + 2)
        flag_line.wait(0, step)
        if step < 2:
            flag_line.start(0, step + 1)
        share(flag_line, flags_all, 0, step, twin_steps, True)
        if step == 0:
            for part in range(2):
                cot_line.wait(part, 2)
            ours = cot_all.at[pl.ds(pair * 4, 4)]
            twin_cot = links.start(ours, ours, place.twin)

    for copy in twin_rows + twin_flags + [twin_cot] + forwarded:
        copy.wait_recv()
    for comes, copy in twin_steps:
        pl.when(comes)(copy.wait_recv)
    for copy in keep_own:
        copy.wait()
    links.finish()


def head(x, cot, small, qkv, out, expert_in, expert_out, noise, ids):
    rows, width = x.shape
    depth = qkv.shape[0]
    count = expert_in.shape[0] // 2
    shape = jax.ShapeDtypeStruct
    anywhere = pl.BlockSpec(memory_space=pl.ANY)
    vmem = pl.BlockSpec(memory_space=pltpu.VMEM)
    return pl.pallas_call(
        head_kernel,
        out_shape=(
            shape((2, TALL, depth), BF),
            shape((width, 3 * width), BF),
            shape((width, width), BF),
            shape((rows, width), BF),
            shape((rows, 3 * width), BF),
            shape((rows, width), BF),
            shape((rows, width), F32),
            shape((TALL, rows), F32),
            shape((8, rows, width), BF),
            shape((8, TALL, rows), BF),
            shape((8, rows, width), BF),
            shape((count,) + expert_in.shape[1:], BF),
            shape((count,) + expert_out.shape[1:], BF),
        ),
        in_specs=[vmem] * 3 + [anywhere] * 4 + [vmem] * 2,
        out_specs=(vmem,) * 8 + (anywhere,) * 5,
        scratch_shapes=[
            pltpu.VMEM((rows, width), BF),
            pltpu.VMEM((TALL, rows), BF),
            pltpu.SemaphoreType.DMA((96,)),
            pltpu.SemaphoreType.DMA((96,)),
            pltpu.SemaphoreType.DMA((4,)),
        ],
        compiler_params=pltpu.CompilerParams(vmem_limit_bytes=BIG, collective_id=1, has_side_effects=True),
        cost_estimate=pl.CostEstimate(flops=8 * 10**9, bytes_accessed=3 * 10**7, transcendentals=10**6),
        name="head",
    )(x, cot, small, qkv, out, expert_in, expert_out, noise, ids)


def expert_kernel(
    place_ref, flag_ref, rows_all, cot_all, own_in, got_in, own_out, got_out,
    total_all, back_all, gate_ref, grad_in, grad_out,
    inner, outer, picked, grads, gate, active, hidden_grad, made, made_back, made_gate, ranks,
    rows_buf, cot_buf, total_buf, back_buf, stage_in, stage_out, load_sem, store_sem, fetch_sem, put_sem, old_sem,
):
    blocks, length, width = cot_all.shape
    count = got_in.shape[0]
    depth = got_in.shape[1]
    pair, shard = place_ref[0], place_ref[1]
    experts = 2 * count

    def loads(expert):
        slot = expert % 2
        mine = pl.ds(pl.multiple_of(shard * depth, LANES), depth)
        other = pl.ds(pl.multiple_of((1 - shard) * depth, LANES), depth)
        index = pair * count + expert
        return (
            pltpu.make_async_copy(own_in.at[index], inner.at[slot, mine, :], load_sem.at[slot, 0]),
            pltpu.make_async_copy(got_in.at[expert], inner.at[slot, other, :], load_sem.at[slot, 1]),
            pltpu.make_async_copy(own_out.at[index], outer.at[slot, :, mine], load_sem.at[slot, 2]),
            pltpu.make_async_copy(got_out.at[expert], outer.at[slot, :, other], load_sem.at[slot, 3]),
        )

    def stores(expert):
        slot = expert % 2
        return (
            pltpu.make_async_copy(stage_in.at[slot], grad_in.at[expert], store_sem.at[slot, 0]),
            pltpu.make_async_copy(stage_out.at[slot], grad_out.at[expert], store_sem.at[slot, 1]),
        )

    def fetches(block):
        slot = block % 2
        return (
            pltpu.make_async_copy(rows_all.at[block], rows_buf.at[slot], fetch_sem.at[slot, 0]),
            pltpu.make_async_copy(cot_all.at[block], cot_buf.at[slot], fetch_sem.at[slot, 1]),
        )

    def puts(block):
        slot = block % 2
        return (
            pltpu.make_async_copy(total_buf.at[slot], total_all.at[block], put_sem.at[slot, 0]),
            pltpu.make_async_copy(back_buf.at[slot], back_all.at[block], put_sem.at[slot, 1]),
        )

    def start(copies):
        for copy in copies:
            copy.start()

    def wait(copies):
        for copy in copies:
            copy.wait()

    def reload(pairs):
        copies = [pltpu.make_async_copy(source, target, old_sem.at[n]) for n, (source, target) in enumerate(pairs)]
        start(copies)
        wait(copies)

    start(fetches(0) + fetches(1) + loads(0))
    ahead = lax.broadcasted_iota(jnp.int32, (length, length), 0)
    behind = lax.broadcasted_iota(jnp.int32, (length, length), 1)
    order = jnp.where(behind < ahead, 1.0, jnp.where(behind == ahead, FAR, 0.0)).astype(BF)
    for block in range(blocks):
        ranks[block] = contract_cols(flag_ref[block], order) - FAR

    def line(expert):
        return pl.ds(experts + pair * count + expert, 1)

    passes = []
    for expert in range(count):
        highest = ranks[0, line(expert), :]
        for block in range(1, blocks):
            highest = jnp.maximum(highest, ranks[block, line(expert), :])
        passes.append((jnp.maximum(jnp.max(highest), -1.0).astype(jnp.int32) + TILE) // TILE)
    rounds = jnp.int32(1)
    for value in passes:
        rounds = jnp.maximum(rounds, value)

    def one_round(step, carry):
        again = step > 0
        slots = lax.broadcasted_iota(jnp.int32, (TILE, length), 0).astype(F32) + (step * TILE).astype(F32)

        def choices(block):
            return jnp.concatenate(
                [(ranks[block, line(expert), :] == slots).astype(BF) for expert in range(count)], 0
            )

        @pl.when(again)
        def _():
            start(fetches(0) + fetches(1) + loads(0))

        lane = lax.broadcasted_iota(jnp.int32, (count * TILE, TALL), 1)
        wanted = lax.broadcasted_iota(jnp.int32, (count * TILE, TALL), 0) // TILE + pair * count
        for block in range(blocks):
            slot = block % 2
            at = pl.ds(block * TILE, TILE)
            choose = choices(block)
            columns = jnp.where(lane == wanted, contract_cols(choose, flag_ref[block]), 0.0)
            column = jnp.broadcast_to(jnp.sum(columns, -1, keepdims=True), (count * TILE, LANES))
            wait(fetches(block))
            both = dot(choose, rows_buf[slot]).astype(BF)
            other = dot(choose, cot_buf[slot]).astype(BF)
            for expert in range(count):
                part = slice(expert * TILE, (expert + 1) * TILE)
                picked[expert, at, :] = both[part]
                grads[expert, at, :] = other[part]
                gate[expert, at, :] = column[part]
            if block + 2 < blocks:
                start(fetches(block + 2))

        for expert in range(count):
            slot = expert % 2
            runs = jnp.logical_or(step == 0, passes[expert] > step)
            if expert + 1 < count:
                start(loads(expert + 1))
            wait(loads(expert))

            @pl.when(runs)
            def _():
                def chunk(index, carry):
                    at = pl.ds(pl.multiple_of(index * CHUNK, CHUNK), CHUNK)
                    value = dot(picked[expert, at, :], inner[slot])
                    grad_active = contract_cols(grads[expert, at, :], outer[slot])
                    gate_column = gate[expert, at, 0:1]
                    square = value * value
                    bent = jnp.tanh(ROOT * value * (1.0 + CUBIC * square))
                    plus = 0.5 * (1.0 + bent)
                    bowed = value * plus
                    slope = plus + (0.5 * ROOT) * value * (1.0 - bent * bent) * (1.0 + (3.0 * CUBIC) * square)
                    active[at, :] = (bowed * gate_column).astype(BF)
                    back = (grad_active * gate_column * slope).astype(BF)
                    hidden_grad[at, :] = back
                    lane = lax.broadcasted_iota(jnp.int32, (CHUNK, TALL), 1)
                    gate_grad = jnp.sum(grad_active * bowed, -1, keepdims=True)
                    made_gate[expert, at, :] = jnp.where(lane == pair * count + expert, gate_grad, 0.0).astype(BF)
                    made[expert, at, :] = dot(active[at, :], outer[slot]).astype(BF)
                    made_back[expert, at, :] = contract_cols(back, inner[slot]).astype(BF)
                    return carry

                lax.fori_loop(0, blocks * TILE // CHUNK, chunk, 0)

            if expert >= 2:
                before = jnp.logical_or(step == 0, passes[expert - 2] > step)

                @pl.when(before)
                def _():
                    wait(stores(expert - 2))

            @pl.when(runs)
            def _():
                for stage, grad, left, right in (
                    (stage_out, grad_out, active, grads.at[expert]), (stage_in, grad_in, picked.at[expert], hidden_grad),
                ):
                    @pl.when(again)
                    def _():
                        reload([(grad.at[expert], stage.at[slot])])

                    for begin in range(0, left.shape[1], CHUNK):
                        at = pl.ds(begin, CHUNK)
                        value = contract_rows(left[:, at], right[...])
                        old = stage[slot, at, :].astype(F32)
                        stage[slot, at, :] = (value + jnp.where(again, old, 0.0)).astype(BF)
                start(stores(expert))

        for block in range(blocks):
            slot = block % 2
            at = pl.ds(block * TILE, TILE)
            choose = choices(block)
            if block >= 2:
                wait(puts(block - 2))

            def joined(source):
                return jnp.concatenate([source[expert, at, :] for expert in range(count)], 0)

            @pl.when(again)
            def _():
                reload([(total_all.at[block], rows_buf.at[0]), (back_all.at[block], rows_buf.at[1])])

            for target, source, old in ((total_buf, made, 0), (back_buf, made_back, 1)):
                target[slot] = contract_rows(choose, joined(source)).astype(BF)

                @pl.when(again)
                def _():
                    target[slot] = (target[slot].astype(F32) + rows_buf[old].astype(F32)).astype(BF)

            start(puts(block))
            gates = contract_rows(joined(made_gate), choose)
            gate_ref[block] = (gates + jnp.where(again, gate_ref[block].astype(F32), 0.0)).astype(BF)
        for block in range(blocks - 2, blocks):
            wait(puts(block))
        for expert in range(count - 2, count):

            @pl.when(jnp.logical_or(step == 0, passes[expert] > step))
            def _():
                wait(stores(expert))

        return carry

    lax.fori_loop(0, rounds, one_round, 0)


def expert_pass(place, rows, flags, cot, own_in, got_in, own_out, got_out):
    blocks, length, width = cot.shape
    count, _, hidden = got_in.shape
    capacity = blocks * TILE
    shape = jax.ShapeDtypeStruct
    anywhere = pl.BlockSpec(memory_space=pl.ANY)
    vmem = pl.BlockSpec(memory_space=pltpu.VMEM)
    return pl.pallas_call(
        expert_kernel,
        out_shape=(
            shape((blocks, length, width), BF),
            shape((blocks, length, width), BF),
            shape((blocks, TALL, length), BF),
            shape((count, width, hidden), BF),
            shape((count, hidden, width), BF),
        ),
        in_specs=[pl.BlockSpec(memory_space=pltpu.SMEM), vmem] + [anywhere] * 6,
        out_specs=(anywhere, anywhere, vmem, anywhere, anywhere),
        scratch_shapes=[
            pltpu.VMEM((2, width, hidden), BF),
            pltpu.VMEM((2, hidden, width), BF),
            pltpu.VMEM((count, capacity, width), BF),
            pltpu.VMEM((count, capacity, width), BF),
            pltpu.VMEM((count, capacity, LANES), F32),
            pltpu.VMEM((capacity, hidden), BF),
            pltpu.VMEM((capacity, hidden), BF),
            pltpu.VMEM((count, capacity, width), BF),
            pltpu.VMEM((count, capacity, width), BF),
            pltpu.VMEM((count, capacity, TALL), BF),
            pltpu.VMEM((blocks, TALL, length), F32),
            pltpu.VMEM((2, length, width), BF),
            pltpu.VMEM((2, length, width), BF),
            pltpu.VMEM((2, length, width), BF),
            pltpu.VMEM((2, length, width), BF),
            pltpu.VMEM((2, width, hidden), BF),
            pltpu.VMEM((2, hidden, width), BF),
            pltpu.SemaphoreType.DMA((2, 4)),
            pltpu.SemaphoreType.DMA((2, 2)),
            pltpu.SemaphoreType.DMA((2, 2)),
            pltpu.SemaphoreType.DMA((2, 2)),
            pltpu.SemaphoreType.DMA((2,)),
        ],
        compiler_params=pltpu.CompilerParams(vmem_limit_bytes=BIG),
        cost_estimate=pl.CostEstimate(flops=50 * 10**9, bytes_accessed=5 * 10**7, transcendentals=10**6),
        name="experts",
    )(place, flags, rows, cot, own_in, got_in, own_out, got_out)


def back_middle(at, moe, gates, cot, middle, rows, probs, flags, small_ref, sums):
    experts = TALL // 2
    row = lax.broadcasted_iota(jnp.int32, flags.shape, 0)
    chosen = jnp.where(row < experts, pltpu.roll(flags, experts, 0), 0.0)
    asked = gates * chosen
    grad_logits = probs * (asked - jnp.sum(probs * asked, 0, keepdims=True))
    coarse = grad_logits.astype(BF)
    fine = (grad_logits - coarse.astype(F32)).astype(BF)
    router = router_rows(small_ref)
    sums[4] = sums[4] + dot(coarse, rows) + dot(fine, rows)
    grad = moe + contract_rows(coarse, router) + contract_rows(fine, router)
    unit, inverse = norm_parts(middle)
    sums[2] = sums[2] + jnp.sum(grad * unit, 0, keepdims=True)
    sums[3] = sums[3] + jnp.sum(grad, 0, keepdims=True)
    return cot + norm_back(grad, unit, inverse, gain_row(small_ref, experts, 2))


def back_heads(at, double, grad_proj, packed_ref, out_ref, stacked):
    width = grad_proj.shape[1]
    group = 3 * HEAD_DIM
    scale = HEAD_DIM ** (-0.5)
    lanes = lax.broadcasted_iota(jnp.int32, (PAD, group), 1) // HEAD_DIM
    made = []
    packed = packed_ref[at, pl.ds(double * 6 * group, 6 * group)]
    for side in range(2):
        query, keys, values = (packed[:, (3 * side + k) * group : (3 * side + k + 1) * group] for k in range(3))
        index = double * 2 + side
        grad_att = contract_cols(grad_proj, out_ref[pl.ds(index * group, group), :]).astype(BF)
        outs = [jnp.zeros((PAD, group), F32) for _ in range(3)]
        for head in range(3):
            mask = lanes == head
            probs = head_probs(jnp.where(mask, query, jnp.zeros_like(query)), keys, scale)
            part = jnp.where(mask, grad_att, jnp.zeros_like(grad_att))
            grad_weights = contract_cols(part, values)
            inner_sum = jnp.sum(probs * grad_weights, -1, keepdims=True)
            grad_scores = (probs * (grad_weights - inner_sum)).astype(BF)
            outs[0] = jnp.where(mask, dot(grad_scores, keys), outs[0])
            outs[1] = jnp.where(mask, contract_rows(grad_scores, query), outs[1])
            outs[2] = jnp.where(mask, contract_rows(probs.astype(BF), grad_att), outs[2])
        made += [outs[0] * scale, outs[1] * scale, outs[2]]
    stacked[at, pl.ds(double * 6 * group, 6 * group)] = jnp.concatenate(made, 1).astype(BF)


def back_kernel(
    moe_ref, gate_ref, cot_ref, x_ref, middle_ref, rows_ref, flag_ref, prob_ref, attended_ref, packed_ref, normed_ref,
    small_ref, qkv_ref, out_ref,
    tokens_ref, grad_qkv, grad_out, grad_small,
    stacked, projected,
):
    rows, width = x_ref.shape
    experts = TALL // 2
    sums = [jnp.zeros((1, width), F32) for _ in range(4)] + [jnp.zeros((TALL, width), F32)]
    for image in range(rows // PAD):
        at = pl.ds(image * PAD, PAD)
        cols = slice(image * PAD, (image + 1) * PAD)
        grad_middle = back_middle(
            at, moe_ref[at, :].astype(F32), gate_ref[:, cols].astype(F32), cot_ref[at, :].astype(F32),
            middle_ref[at, :], rows_ref[at, :], prob_ref[:, cols], flag_ref[:, cols].astype(F32), small_ref, sums,
        )
        grad_proj = grad_middle.astype(BF)
        projected[at, :] = grad_proj
        for double in range(width // (6 * HEAD_DIM)):
            back_heads(at, double, grad_proj, packed_ref, out_ref, stacked)
        grad = contract_cols(stacked[at, :], qkv_ref[...])
        unit, inverse = norm_parts(x_ref[at, :].astype(F32))
        sums[0] = sums[0] + jnp.sum(grad * unit, 0, keepdims=True)
        sums[1] = sums[1] + jnp.sum(grad, 0, keepdims=True)
        tokens_ref[at, :] = (grad_middle + norm_back(grad, unit, inverse, gain_row(small_ref, experts, 0))).astype(BF)
    grad_small[...] = jnp.concatenate([sums[4][0:experts]] + sums[:4] + [jnp.zeros((4, width), F32)], 0).astype(BF)
    grad_out[...] = contract_rows(attended_ref[...], projected[...]).astype(BF)
    for third in range(3):
        cols = pl.ds(third * width, width)
        grad_qkv[:, cols] = contract_rows(normed_ref[...], stacked[:, cols]).astype(BF)


def back(moe, gates, cot, x, middle, sent, flags, prob, attended, packed, normed, small, qkv, out):
    rows, width = x.shape
    shape = jax.ShapeDtypeStruct
    return pl.pallas_call(
        back_kernel,
        out_shape=(
            shape((rows, width), BF),
            shape((width, 3 * width), BF),
            shape((width, width), BF),
            shape((TALL, width), BF),
        ),
        scratch_shapes=[pltpu.VMEM((rows, 3 * width), BF), pltpu.VMEM((rows, width), BF)],
        compiler_params=pltpu.CompilerParams(vmem_limit_bytes=BIG),
        cost_estimate=pl.CostEstimate(flops=16 * 10**9, bytes_accessed=2 * 10**7, transcendentals=10**6),
        name="back",
    )(moe, gates, cot, x, middle, sent, flags, prob, attended, packed, normed, small, qkv, out)


ORDER = [[('x', 0), ('x', 1)], [('x', 2)], [('a', 0), ('x', 3), ('a', 1), ('x', 4), ('y', 0), ('x', 5)], [], [], [], [], [('b', 0), ('x', 6)], [('da', 0), ('b', 1), ('y', 1), ('da', 2), ('da', 3), ('y', 2), ('dl', 0), ('da', 1), ('x', 7)], [('dl', 2), ('y', 3), ('x', 8), ('dl', 3), ('db', 0), ('x', 9), ('y', 4), ('db', 2), ('y', 5), ('y', 6), ('dl', 1), ('y', 7), ('ds', 0), ('db', 3), ('c', 0), ('y', 8), ('s', 0), ('x', 10), ('c', 1), ('ds', 2), ('y', 9), ('s', 1), ('y', 10), ('s', 2), ('db', 1), ('ds', 3), ('dt', 0), ('ds', 1), ('dt', 2), ('x', 11), ('y', 11)], [('s', 3), ('dt', 3), ('dt', 1)]]


class LineScatter:
    def __init__(self, links, place, sums, up, down):
        self.links, self.place = links, place
        self.sums, self.up, self.down = sums, up, down
        self.copies = {}

    def ways(self, step):
        t = self.place.tensor
        return (
            ("up", self.up, t + 3 - step, t <= step, t >= 1, self.place.above),
            ("down", self.down, t - 3 + step, t >= 3 - step, t <= 2, self.place.below),
        )

    def send(self, part, step):
        for name, got, slot, sends, comes, device in self.ways(step):
            slot = jnp.clip(slot, 0, 3)
            if step > 0:
                before = self.copies[name, part, step - 1]

                @pl.when(sends & comes)
                def _():
                    before.wait_recv()
                    ref = self.sums(slot, part)
                    ref[...] = (ref[...].astype(F32) + got(step - 1, part)[...].astype(F32)).astype(BF)

            copy = self.links.copy(self.sums(slot, part), got(step, part), device)
            pl.when(sends)(copy.start)
            self.links.sent.append((sends, copy))
            self.copies[name, part, step] = copy

    def finish(self, part, total):
        total[...] = self.sums(self.place.tensor, part)[...].astype(F32)
        for name, got, slot, sends, comes, device in self.ways(2):
            copy = self.copies[name, part, 2]

            @pl.when(comes)
            def _():
                copy.wait_recv()
                total[...] += got(2, part)[...].astype(F32)


def tail_kernel(
    back_all, gate_all, total_all, grads_in, grads_out, rows_all, flags_all,
    cot_ref, x_ref, middle_ref, prob_ref, attended_ref, packed_ref, normed_ref, small_ref, qkv_ref, out_ref,
    mixed_ref, tokens_ref, dense_ref, grad_small, final_in, final_out, beside_in, beside_out,
    back_sum, back_got, back_up, back_down, gate_sum, gate_got, gate_up, gate_down,
    total_sum, total_got, total_up, total_down, moe, gates, rows_ref, flag_ref, projected, stacked,
    chunks, core_got, across_sent, across_got, line_sum, line_got, side_sum, side_got, line_final,
    own_in, own_out, across_in, across_out, read_in, read_out, half_in, half_out, mine_in, mine_out, both_in, both_out,
    small_sent, small_core, small_half, small_across, small_side, small_beside, small_line_sent, small_line,
    send, recv, local_sem,
):
    place = Place()
    links = Links(send, recv)
    rows, width = x_ref.shape
    experts = TALL // 2
    count = grads_in.shape[0]
    depth = width // 2
    shard, pair, side, tensor = place.shard, place.pair, place.side, place.tensor
    mine = pair * 4 + tensor
    place.greet(True)
    ours, theirs = pl.ds(pair * 4, 4), pl.ds((1 - pair) * 4, 4)

    locals_ = [
        pltpu.make_async_copy(back_all.at[ours], back_sum, local_sem.at[0]),
        pltpu.make_async_copy(gate_all.at[ours], gate_sum, local_sem.at[1]),
        pltpu.make_async_copy(total_all.at[ours], total_sum, local_sem.at[2]),
        pltpu.make_async_copy(rows_all.at[mine], rows_ref, local_sem.at[3]),
        pltpu.make_async_copy(flags_all.at[mine], flag_ref, local_sem.at[4]),
    ]
    for copy in locals_:
        copy.start()
    from_twin = [links.start(gate_all.at[theirs], gate_got, place.twin)]
    for part in range(2):
        at = pl.ds(part * PAD, PAD)
        from_twin.append(links.start(back_all.at[theirs, at, :], back_got.at[:, at, :], place.twin))
    from_twin.append(links.start(total_all.at[theirs], total_got, place.twin))

    here = pl.ds(pl.multiple_of(shard * depth, LANES), depth)
    there = pl.ds(pl.multiple_of((1 - shard) * depth, LANES), depth)
    hidden = grads_in.shape[2]
    tall, wide = depth // 2, hidden // 2
    pieces = []
    for expert in range(1, count):
        for half in range(2):
            at = pl.ds(half * tall, tall)
            pieces.append((
                grads_in.at[expert, pl.ds(pl.multiple_of((1 - shard) * depth + half * tall, TALL), tall), :],
                grads_in.at[expert, pl.ds(pl.multiple_of(shard * depth + half * tall, TALL), tall), :],
                across_in.at[expert - 1, at, :], beside_in.at[expert - 1, at, :],
                final_in.at[pair * count + expert, at, :], own_in.at[at, :], read_in.at[at, :],
            ))
        for half in range(2):
            at = pl.ds(half * wide, wide)
            pieces.append((
                grads_out.at[expert, at, there], grads_out.at[expert, at, here],
                across_out.at[expert - 1, at, :], beside_out.at[expert - 1, at, :],
                final_out.at[pair * count + expert, at, :], own_out.at[at, :], read_out.at[at, :],
            ))
    loads = [pltpu.make_async_copy(piece[1], piece[5], local_sem.at[8 + m]) for m, piece in enumerate(pieces)]
    at_across, at_beside, at_twin, kept = {}, {}, [], []
    started = [0]

    def add(target, source):
        target[...] = (target[...].astype(F32) + source[...].astype(F32)).astype(BF)

    def keep(source, target):
        copy = pltpu.make_async_copy(source, target, local_sem.at[32 + len(kept)])
        copy.start()
        kept.append(copy)

    def send_across():
        m = started[0]
        if m < len(pieces):
            at_across[m] = links.start(pieces[m][0], pieces[m][2], place.across)
            started[0] += 1

    def take_across(m):
        at_across[m].wait_recv()
        send_across()
        loads[m].wait()
        add(pieces[m][2], pieces[m][5])
        at_beside[m] = links.start(pieces[m][2], pieces[m][3], place.beside)
        if m + 4 < len(pieces):
            loads[m + 4].start()

    def take_beside(m):
        at_beside[m].wait_recv()
        load = pltpu.make_async_copy(pieces[m][3], pieces[m][6], local_sem.at[5])
        load.start()
        at_beside[m].wait_send()
        links.skip(at_beside[m])
        load.wait()
        add(pieces[m][2], pieces[m][6])
        at_twin.append(links.start(pieces[m][2], pieces[m][4], place.twin))
        keep(pieces[m][2], pieces[m][4])

    our_half = pl.ds(pl.multiple_of(side * wide, LANES), wide)
    other_half = pl.ds(pl.multiple_of((1 - side) * wide, LANES), wide)
    first = (
        (grads_in.at[0, :, other_half], grads_in.at[0, :, our_half], half_in, mine_in,
         half_in.at[there, :], half_in.at[here, :], both_in,
         final_in.at[pair * count, :, our_half], final_in.at[pair * count, :, other_half]),
        (grads_out.at[0, other_half, :], grads_out.at[0, our_half, :], half_out, mine_out,
         half_out.at[:, there], half_out.at[:, here], both_out,
         final_out.at[pair * count, our_half, :], final_out.at[pair * count, other_half, :]),
    )
    first_loads = [pltpu.make_async_copy(item[1], item[3], local_sem.at[6 + q]) for q, item in enumerate(first)]
    first_beside, first_across, first_back = {}, {}, {}

    def first_send(q):
        first_loads[q].start()
        first_beside[q] = links.start(first[q][0], first[q][2], place.beside)

    def first_sum(q):
        first_beside[q].wait_recv()
        first_loads[q].wait()
        add(first[q][2], first[q][3])
        first_across[q] = links.start(first[q][4], first[q][6], place.across)

    def first_total(q):
        first_across[q].wait_recv()
        add(first[q][6], first[q][5])
        first_back[q] = links.start(first[q][6], first[q][7], place.beside)
        at_twin.append(links.start(first[q][6], first[q][7], place.twin))
        keep(first[q][6], first[q][7])

    def first_share(q):
        first_back[q].wait_recv()
        at_twin.append(links.start(first[q][8], first[q][8], place.twin))

    share = depth // 2
    piece = share // 4
    stage = {}

    def dense_core(k):
        stage["core", k] = []
        for owner in range(2):
            source = chunks.at[k, pl.ds(pl.multiple_of(owner * depth + (1 - pair) * share, TALL), share), :]
            stage["core", k].append(links.start(source, core_got.at[k, owner], place.twin))

    def core_sum(k, owner):
        at = pl.ds(pl.multiple_of(owner * depth + pair * share, TALL), share)
        return chunks[k, at, :].astype(F32) + core_got[k, owner].astype(F32)

    def dense_across(k):
        for copy in stage["core", k]:
            copy.wait_recv()
        across_sent[k] = core_sum(k, 1 - shard).astype(BF)
        stage["across", k] = links.start(across_sent.at[k], across_got.at[k], place.across)

    def around(offset):
        return (shard, place.head, lax.rem(tensor + offset, 4))

    def dense_line(k):
        stage["across", k].wait_recv()
        line_sum[k] = (core_sum(k, shard) + across_got[k].astype(F32)).astype(BF)
        stage["line", k] = []
        for offset in (2, 1, 3):
            at = pl.ds(pl.multiple_of(lax.rem(tensor + offset, 4) * piece, TALL), piece)
            stage["line", k].append(links.start(line_sum.at[k, at, :], line_got.at[k, offset - 1], around(offset)))

    def dense_beside(k):
        for copy in stage["line", k]:
            copy.wait_recv()
        at = pl.ds(pl.multiple_of(tensor * piece, TALL), piece)
        value = line_sum[k, at, :].astype(F32)
        for offset in range(3):
            value = value + line_got[k, offset].astype(F32)
        side_sum[k] = value.astype(BF)
        stage["beside", k] = links.start(side_sum.at[k], side_got.at[k], place.beside)

    def dense_spread(k):
        stage["beside", k].wait_recv()
        line_final[k] = (side_sum[k].astype(F32) + side_got[k].astype(F32)).astype(BF)
        target = dense_ref.at[
            pl.ds(pl.multiple_of(pair * share + tensor * piece, TALL), piece), pl.ds(k * width, width)
        ]
        stage["spread", k] = [links.start(line_final.at[k], target, around(offset)) for offset in (2, 1, 3)]
        stage["keep", k] = pltpu.make_async_copy(line_final.at[k], target, local_sem.at[24 + k])
        stage["keep", k].start()

    def dense_twin(k):
        for copy in stage["spread", k]:
            copy.wait_recv()
        stage["keep", k].wait()
        block = dense_ref.at[pl.ds(pl.multiple_of(pair * share, TALL), share), pl.ds(k * width, width)]
        stage["twin", k] = links.start(block, block, place.twin)

    def small_core_stage():
        small_core_copy.wait_recv()
        other = pl.ds(pl.multiple_of((1 - shard) * depth, LANES), depth)
        small_half[...] = small_sent[:, other] + small_core[:, other]
        stage["small", 1] = links.start(small_half, small_across, place.across)

    def small_across_stage():
        stage["small", 1].wait_recv()
        own = pl.ds(pl.multiple_of(shard * depth, LANES), depth)
        small_side[...] = small_sent[:, own] + small_core[:, own] + small_across[...]
        stage["small", 2] = links.start(small_side, small_beside, place.beside)

    def small_beside_stage():
        stage["small", 2].wait_recv()
        small_line_sent[...] = small_side[...] + small_beside[...]
        stage["small", 3] = [
            links.start(small_line_sent, small_line.at[offset - 1], around(offset)) for offset in (2, 1, 3)
        ]

    def small_line_stage():
        for copy in stage["small", 3]:
            copy.wait_recv()
        grad_small[...] = small_line_sent[...] + small_line[0] + small_line[1] + small_line[2]

    def slots(array):
        def view(slot, part):
            return array.at[slot, pl.ds(part * PAD, PAD), :]

        return view

    back_line = LineScatter(links, place, slots(back_sum), slots(back_up), slots(back_down))
    total_line = LineScatter(links, place, slots(total_sum), slots(total_up), slots(total_down))
    gate_line = LineScatter(
        links, place, lambda slot, part: gate_sum.at[slot], lambda step, part: gate_up.at[step],
        lambda step, part: gate_down.at[step],
    )

    steps = {
        "x": take_across, "y": take_beside, "a": first_sum, "b": first_total, "c": first_share,
        "da": dense_across, "dl": dense_line, "db": dense_beside, "ds": dense_spread, "dt": dense_twin,
        "s": lambda index: (small_core_stage, small_across_stage, small_beside_stage, small_line_stage)[index](),
    }

    def go(slot):
        for name, index in ORDER[slot]:
            steps[name](index)

    first_send(0)
    for _ in range(3):
        send_across()
    first_send(1)
    for m in range(4):
        loads[m].start()
    locals_[1].wait()
    from_twin[0].wait_recv()
    add(gate_sum, gate_got)
    gate_line.send(0, 0)
    locals_[0].wait()
    for part in range(2):
        from_twin[1 + part].wait_recv()
        at = pl.ds(part * PAD, PAD)
        for slot in range(4):
            add(back_sum.at[slot, at, :], back_got.at[slot, at, :])
        back_line.send(part, 0)
    locals_[2].wait()
    from_twin[3].wait_recv()
    for slot in range(4):
        add(total_sum.at[slot], total_got.at[slot])
    go(0)
    gate_line.send(0, 1)
    for part in range(2):
        back_line.send(part, 1)
    go(1)
    gate_line.send(0, 2)
    for part in range(2):
        back_line.send(part, 2)
    go(2)
    for part in range(2):
        total_line.send(part, 0)
    gate_line.finish(0, gates)
    locals_[3].wait()
    locals_[4].wait()

    sums = [jnp.zeros((1, width), F32) for _ in range(4)] + [jnp.zeros((TALL, width), F32)]
    for image in range(2):
        at = pl.ds(image * PAD, PAD)
        cols = slice(image * PAD, (image + 1) * PAD)
        back_line.finish(image, moe.at[at, :])
        grad = back_middle(
            at, moe[at, :], gates[:, cols], cot_ref[at, :].astype(F32), middle_ref[at, :], rows_ref[at, :],
            prob_ref[:, cols], flag_ref[:, cols].astype(F32), small_ref, sums,
        )
        moe[at, :] = grad
        projected[at, :] = grad.astype(BF)
    go(3)
    chunks[0] = contract_rows(attended_ref[...], projected[...]).astype(BF)
    dense_core(0)
    go(4)
    for image in range(2):
        at = pl.ds(image * PAD, PAD)
        back_heads(at, 0, projected[at, :], packed_ref, out_ref, stacked)
        if image == 0:
            go(5)
    chunks[1] = contract_rows(normed_ref[...], stacked[:, pl.ds(0, width)]).astype(BF)
    dense_core(1)
    for part in range(2):
        total_line.send(part, 1)
    go(6)
    for image in range(2):
        at = pl.ds(image * PAD, PAD)
        back_heads(at, 1, projected[at, :], packed_ref, out_ref, stacked)
        if image == 0:
            go(7)
    for k in (2, 3):
        chunks[k] = contract_rows(normed_ref[...], stacked[:, pl.ds((k - 1) * width, width)]).astype(BF)
        dense_core(k)
    for part in range(2):
        total_line.send(part, 2)
    go(8)
    for image in range(2):
        at = pl.ds(image * PAD, PAD)
        grad = contract_cols(stacked[at, :], qkv_ref[...])
        unit, inverse = norm_parts(x_ref[at, :].astype(F32))
        sums[0] = sums[0] + jnp.sum(grad * unit, 0, keepdims=True)
        sums[1] = sums[1] + jnp.sum(grad, 0, keepdims=True)
        tokens_ref[at, :] = (
            moe[at, :] + norm_back(grad, unit, inverse, gain_row(small_ref, experts, 0))
        ).astype(BF)
    small_sent[...] = jnp.concatenate([sums[4][0:experts]] + sums[:4] + [jnp.zeros((4, width), F32)], 0)
    small_core_copy = links.start(small_sent, small_core, place.twin)
    go(9)
    for part in range(2):
        at = pl.ds(part * PAD, PAD)
        total_line.finish(part, moe.at[at, :])
        mixed_ref[at, :] = (middle_ref[at, :] + moe[at, :]).astype(BF)
    go(10)
    for copy in at_twin + [stage["twin", k] for k in range(4)]:
        copy.wait_recv()
    for copy in kept:
        copy.wait()
    links.finish()


def tail(back_all, gate_all, total_all, grads_in, grads_out, rows_all, flags_all, cot, x, middle, prob, attended, packed, normed, small, qkv, out):
    rows, width = x.shape
    count, _, hidden = grads_in.shape
    depth = width // 2
    shape = jax.ShapeDtypeStruct
    anywhere = pl.BlockSpec(memory_space=pl.ANY)
    vmem = pl.BlockSpec(memory_space=pltpu.VMEM)
    share, piece = depth // 2, depth // 8

    def scatter_buffers(tall, wide):
        return [pltpu.VMEM((4, tall, wide), BF)] * 2 + [pltpu.VMEM((3, tall, wide), BF)] * 2

    return pl.pallas_call(
        tail_kernel,
        out_shape=(
            shape((rows, width), BF),
            shape((rows, width), BF),
            shape((depth, 4 * width), BF),
            shape((TALL, depth), F32),
            shape((2 * count, depth, hidden), BF),
            shape((2 * count, hidden, depth), BF),
            shape((count - 1, depth, hidden), BF),
            shape((count - 1, hidden, depth), BF),
        ),
        in_specs=[anywhere] * 7 + [vmem] * 10,
        out_specs=(vmem,) * 4 + (anywhere,) * 4,
        scratch_shapes=scatter_buffers(rows, width)
        + scatter_buffers(TALL, rows)
        + scatter_buffers(rows, width)
        + [
            pltpu.VMEM((rows, width), F32),
            pltpu.VMEM((TALL, rows), F32),
            pltpu.VMEM((rows, width), BF),
            pltpu.VMEM((TALL, rows), BF),
            pltpu.VMEM((rows, width), BF),
            pltpu.VMEM((rows, 3 * width), BF),
            pltpu.VMEM((4, width, width), BF),
            pltpu.VMEM((4, 2, share, width), BF),
            pltpu.VMEM((4, share, width), BF),
            pltpu.VMEM((4, share, width), BF),
            pltpu.VMEM((4, share, width), BF),
            pltpu.VMEM((4, 3, piece, width), BF),
            pltpu.VMEM((4, piece, width), BF),
            pltpu.VMEM((4, piece, width), BF),
            pltpu.VMEM((4, piece, width), BF),
        ]
        + [pltpu.VMEM((depth, hidden), BF), pltpu.VMEM((hidden, depth), BF)]
        + [pltpu.VMEM((count - 1, depth, hidden), BF), pltpu.VMEM((count - 1, hidden, depth), BF)]
        + [pltpu.VMEM((depth, hidden), BF), pltpu.VMEM((hidden, depth), BF)]
        + [pltpu.VMEM((width, hidden // 2), BF), pltpu.VMEM((hidden // 2, width), BF)] * 2
        + [pltpu.VMEM((depth, hidden // 2), BF), pltpu.VMEM((hidden // 2, depth), BF)]
        + [
            pltpu.VMEM((TALL, width), F32),
            pltpu.VMEM((TALL, width), F32),
            pltpu.VMEM((TALL, depth), F32),
            pltpu.VMEM((TALL, depth), F32),
            pltpu.VMEM((TALL, depth), F32),
            pltpu.VMEM((TALL, depth), F32),
            pltpu.VMEM((TALL, depth), F32),
            pltpu.VMEM((3, TALL, depth), F32),
            pltpu.SemaphoreType.DMA((192,)),
            pltpu.SemaphoreType.DMA((192,)),
            pltpu.SemaphoreType.DMA((48,)),
        ],
        compiler_params=pltpu.CompilerParams(vmem_limit_bytes=BIG, collective_id=2, has_side_effects=True),
        cost_estimate=pl.CostEstimate(flops=16 * 10**9, bytes_accessed=5 * 10**7, transcendentals=10**6),
        name="tail",
    )(back_all, gate_all, total_all, grads_in, grads_out, rows_all, flags_all, cot, x, middle, prob, attended, packed, normed, small, qkv, out)


class Comm:
    def __init__(self):
        self.sizes = tuple(lax.axis_size(axis) for axis in AXES)
        self.shard = lax.axis_index("shard")
        self.head = lax.axis_index("heads")
        self.tensor = lax.axis_index("tensor")
        self.pair = self.head % 2

    def move(self, value, step):
        shards, heads, tensors = self.sizes
        pairs = []
        for s in range(shards):
            for h in range(heads):
                for t in range(tensors):
                    to = step(s, h, t)
                    if 0 <= to[2] < tensors:
                        source = (s * heads + h) * tensors + t
                        pairs.append((source, (to[0] * heads + to[1]) * tensors + to[2]))
        return lax.ppermute(value, AXES, pairs)

    def over_core(self, value):
        return self.move(value, lambda s, h, t: (s, h ^ 1, t))

    def over_heads(self, value):
        return self.move(value, lambda s, h, t: (s, (h + 2) % 4, t))

    def over_shard(self, value):
        return self.move(value, lambda s, h, t: (1 - s, h, t))

    def up(self, value):
        return self.move(value, lambda s, h, t: (s, h, t + 1))

    def down(self, value):
        return self.move(value, lambda s, h, t: (s, h, t - 1))

    def halves(self, value, index, axis):
        size = value.shape[axis] // 2
        mine = lax.dynamic_slice_in_dim(value, index * size, size, axis)
        other = lax.dynamic_slice_in_dim(value, (1 - index) * size, size, axis)
        return mine, other

    def join(self, mine, other, index, axis):
        first = jnp.where(index == 0, mine, other)
        second = jnp.where(index == 0, other, mine)
        return jnp.concatenate((first, second), axis)

    def gather_shard(self, value, axis):
        if self.sizes[0] != 2:
            return lax.all_gather(value, "shard", axis=axis, tiled=True)
        return self.join(value, self.over_shard(value), self.shard, axis)

    def gather_shard_split(self, value, axis, cut):
        if self.sizes[0] != 2:
            return lax.all_gather(value, "shard", axis=axis, tiled=True)
        mine, _ = self.halves(value, self.pair, cut)
        got = self.over_shard(mine)
        both = self.join(got, self.over_core(got), self.pair, cut)
        return self.join(value, both, self.shard, axis)

    def scatter_shard(self, value, axis):
        if self.sizes[0] != 2:
            return lax.psum_scatter(value.astype(BF), "shard", scatter_dimension=axis, tiled=True).astype(F32)
        mine, other = self.halves(value, self.shard, axis)
        return mine.astype(F32) + self.over_shard(other.astype(BF)).astype(F32)

    def scatter_core(self, value, axis):
        mine, other = self.halves(value, self.pair, axis)
        return mine.astype(F32) + self.over_core(other.astype(BF)).astype(F32)

    def scatter_heads(self, value, axis):
        mine, other = self.halves(value, self.head // 2, axis)
        return mine.astype(F32) + self.over_heads(other.astype(BF)).astype(F32)

    def line_gather(self, value):
        ups, downs = [value], [value]
        for _ in range(3):
            ups.append(self.up(ups[-1]))
            downs.append(self.down(downs[-1]))
        out = [value]
        for back in (1, 2, 3):
            out.append(jnp.where(self.tensor >= back, ups[back], downs[4 - back]))
        return out

    def line_scatter(self, parts):
        high, low = parts[1].astype(BF), parts[3].astype(BF)
        high = (parts[2].astype(F32) + self.up(high).astype(F32)).astype(BF)
        low = (parts[2].astype(F32) + self.down(low).astype(F32)).astype(BF)
        high = (parts[3].astype(F32) + self.up(high).astype(F32)).astype(BF)
        low = (parts[1].astype(F32) + self.down(low).astype(F32)).astype(BF)
        return parts[0].astype(F32) + self.up(high).astype(F32) + self.down(low).astype(F32)

    def join_slots(self, values):
        own = jnp.zeros((4,) + values[0].shape, values[0].dtype)
        for back, value in enumerate(values):
            own = lax.dynamic_update_index_in_dim(own, value, (self.tensor + 4 - back) % 4, 0)
        return self.join(own, self.over_core(own), self.pair, 0)

    def collect(self, value):
        mine, other = self.halves(value, self.pair, 0)
        mine = mine.astype(F32) + self.over_core(other).astype(F32)
        return self.line_scatter(
            [lax.dynamic_index_in_dim(mine, (self.tensor + 4 - k) % 4, 0, False) for k in range(4)]
        )


def local(
    tokens, ln1_gain, ln1_bias, qkv_weight, out_weight, ln2_gain, ln2_bias, router_weight,
    expert_in, expert_out, route_noise, expert_ids, cotangent,
):
    comm = Comm()
    rows, width = tokens.shape
    experts = expert_in.shape[0]
    images = rows // SEQ
    half = experts // 2
    padded = images * PAD

    def pad(value):
        value = value.reshape(images, SEQ, value.shape[1])
        return jnp.pad(value, ((0, 0), (0, PAD - SEQ), (0, 0))).reshape(padded, value.shape[2])

    def pad_turned(value, tall, fill):
        value = value.reshape(images, SEQ, value.shape[1]).transpose(2, 0, 1)
        value = jnp.pad(value, ((0, tall - value.shape[0]), (0, 0), (0, PAD - SEQ)), constant_values=fill)
        return value.reshape(tall, padded)

    def unpad(value):
        return value.reshape(images, PAD, value.shape[1])[:, :SEQ].reshape(rows, value.shape[1])

    small = jnp.concatenate(
        (router_weight.T, ln1_gain[None], ln1_bias[None], ln2_gain[None], ln2_bias[None]), 0
    )
    small = jnp.pad(small, ((0, TALL - small.shape[0]), (0, 0)))
    cot, x = pad(cotangent), pad(tokens)
    noise, ids = pad_turned(route_noise, TALL, 0), pad_turned(expert_ids, 8, -1)
    place = jnp.stack((comm.pair, comm.shard if comm.sizes[0] == 2 else 0 * comm.shard)).astype(jnp.int32)
    if comm.sizes[0] == 2:
        (
            small, proj_qkv, proj_out, normed_a, packed, attended, middle, prob,
            rows_all, flags_all, grad_rows, got_in, got_out,
        ) = head(x, cot, small, qkv_weight, out_weight, expert_in, expert_out, noise, ids)
        weights = (expert_in, got_in, expert_out, got_out)
    else:
        small = lax.all_gather(small, "shard", axis=1, tiled=True)
        small = small.reshape(TALL, 2, width // 2).transpose(1, 0, 2)
        proj_qkv = lax.all_gather(qkv_weight, "shard", axis=0, tiled=True)
        proj_out = lax.all_gather(out_weight, "shard", axis=0, tiled=True)
        inner = lax.all_gather(lax.dynamic_slice_in_dim(expert_in, comm.pair * half, half, 0), "shard", axis=1, tiled=True)
        outer = lax.all_gather(lax.dynamic_slice_in_dim(expert_out, comm.pair * half, half, 0), "shard", axis=2, tiled=True)
        cut = width // 2
        weights = (
            jnp.concatenate((inner[:, :cut], inner[:, :cut]), 0), inner[:, cut:],
            jnp.concatenate((outer[:, :, :cut], outer[:, :, :cut]), 0), outer[:, :, cut:],
        )
        normed_a, packed, attended, middle, sent, flags, prob = front(x, small, proj_qkv, proj_out, noise, ids)

        def gather(value):
            return comm.join_slots(comm.line_gather(value))

        grad_rows, rows_all, flags_all = gather(cot), gather(sent), gather(flags)
    total, back_all, gate_all, grads_in, grads_out = expert_pass(place, rows_all, flags_all, grad_rows, *weights)

    if comm.sizes[0] == 2:
        mixed, grad_tokens, dense, grad_small, grad_in, grad_outer, _, _ = tail(
            back_all, gate_all, total, grads_in, grads_out, rows_all, flags_all,
            cot, x, middle, prob, attended, packed, normed_a, small, proj_qkv, proj_out,
        )
        dense = dense.astype(F32)
        return (
            unpad(mixed),
            unpad(grad_tokens),
            grad_small[experts],
            grad_small[experts + 1],
            dense[:, width:],
            dense[:, :width],
            grad_small[experts + 2],
            grad_small[experts + 3],
            grad_small[:experts].T,
            grad_in.astype(F32),
            grad_outer.astype(F32),
        )

    def reduce_expert(grad, axis, other):
        part = comm.scatter_shard(grad, axis)
        part = comm.scatter_heads(part, other).astype(BF)
        return comm.join(part, comm.over_heads(part), comm.head // 2, other)

    inner_grads = [reduce_expert(grads_in[e], 0, 1) for e in range(half)]
    outer_grads = [reduce_expert(grads_out[e], 1, 0) for e in range(half)]

    moe_grad = comm.collect(back_all)
    gate_grad = comm.collect(gate_all)
    moe = comm.collect(total)
    mixed = (unpad(middle) + unpad(moe)).astype(BF)
    grad_tokens, grad_qkv, grad_out, grad_small = back(
        moe_grad, gate_grad, cot, x, middle, sent, flags, prob, attended, packed, normed_a, small, proj_qkv, proj_out
    )
    grad_tokens = unpad(grad_tokens)

    grad_small = jnp.pad(grad_small.T, ((0, 0), (0, 128 - TALL)))
    shares = jnp.concatenate((grad_qkv, grad_out, grad_small, jnp.zeros_like(grad_small)), 1)
    shares = comm.scatter_core(shares, 1)
    shares = comm.scatter_shard(shares, 0)
    shares = comm.scatter_heads(shares, 1)
    cut = shares.shape[0] // 4
    rolled = [
        lax.dynamic_slice_in_dim(shares, ((comm.tensor + 4 - k) % 4) * cut, cut, 0) for k in range(4)
    ]
    summed = comm.line_scatter(rolled).astype(BF)
    pieces = comm.line_gather(summed)
    whole = jnp.zeros(shares.shape, BF)
    for k in range(4):
        whole = lax.dynamic_update_slice_in_dim(whole, pieces[k], ((comm.tensor + 4 - k) % 4) * cut, 0)
    whole = comm.join(whole, comm.over_heads(whole), comm.head // 2, 1)
    whole = comm.join(whole, comm.over_core(whole), comm.pair, 1).astype(F32)
    small = whole[:, 4 * width : 4 * width + 128]

    grad_in, grad_outer = jnp.stack(inner_grads, 0), jnp.stack(outer_grads, 0)
    grad_in = comm.join(grad_in, comm.over_core(grad_in), comm.pair, 0).astype(F32)
    grad_outer = comm.join(grad_outer, comm.over_core(grad_outer), comm.pair, 0).astype(F32)
    return (
        mixed,
        grad_tokens,
        small[:, experts],
        small[:, experts + 1],
        whole[:, : 3 * width],
        whole[:, 3 * width : 4 * width],
        small[:, experts + 2],
        small[:, experts + 3],
        small[:, :experts],
        grad_in,
        grad_outer,
    )


def solution(mesh):
    split = P(AXES, None)
    vector, matrix = P("shard"), P("shard", None)
    inner, outer = P(None, "shard", "tensor"), P(None, "tensor", "shard")
    return jax.shard_map(
        local,
        mesh=mesh,
        in_specs=(
            split, vector, vector, matrix, matrix, vector, vector, matrix, inner, outer, split, split, split,
        ),
        out_specs=(
            split, split, vector, vector, matrix, matrix, vector, vector, matrix, inner, outer,
        ),
        check_vma=False,
    )
```

profile of v0, /device:TPU:17, one launch (start us, length us, event | category | flops | bytes accessed | tf_op | source)
XLA Modules:
  0.0 376.6 jit_solution(3252041728136811113)
XLA Ops:
  1.2 0.7 broadcast_in_dim.12
  1.9 0.7 broadcast_in_dim.13
  2.6 0.7 broadcast_in_dim.14
  4.0 0.8 reshape.64
  4.7 0.7 concatenate.3
  6.1 0.7 reshape.65.ids_ref
  6.8 0.8 reshape.62
  7.6 0.7 reshape.63.noise_ref
  8.3 1.2 reshape.58
  9.5 0.9 pad.19
  10.4 1.2 reshape.60
  11.6 0.9 pad.20
  12.4 90.0 %head.1 = (bf16[2,16,384]{2,1,0:T(8,128)(2,1)}, bf16[768,2304]{1,0:T(8,128)(2,1)}, bf16[768,768]{1,0:T(8,128)(2,1)}, bf16[416,768]{1,0:T(8,128)(2,1)}, bf16[416,...) custom-call(bf16[416,768]{1,0:T(8,128)(2,1)} %bitcast.17, ...), custom_call_target="tpu_custom_call" | custom-call | flops 8000000000 | bytes 30000000 | tf_op jit(solution)/shard_map/head/pallas_call | solution.py:411
  102.5 93.9 %experts.1 = (bf16[8,416,768]{2,1,0:T(8,128)(2,1)}, bf16[8,416,768]{2,1,0:T(8,128)(2,1)}, bf16[8,16,416]{2,1,0:T(8,128)(2,1)}, bf16[4,768,768]{2,1,0:T(8,128)(2,1)}, bf16[4,768,768]{2,1,0:T(8,128)(2,1)}) custom-call(s32[2]{0:T(128)} %pad_add_fusion.place_ref, bf16[8,16,416]{2,1,0:T(8,128)(2,1)} %get-tuple-element.35.flag_ref.flags_all, ...), custom_call_target="tpu_custom_call" | custom-call | flops 49999998976 | bytes 50000000 | tf_op jit(solution)/shard_map/experts/pallas_call | solution.py:651
  196.3 161.3 %tail.1 = (bf16[416,768]{1,0:T(8,128)(2,1)}, bf16[416,768]{1,0:T(8,128)(2,1)}, bf16[384,3072]{1,0:T(8,128)(2,1)}, f32[16,384]{1,0:T(8,128)}, bf16[8,384,768]{2,1...) custom-call(bf16[8,416,768]{2,1,0:T(8,128)(2,1)} %get-tuple-element.40.ba, ...), custom_call_target="tpu_custom_call" | custom-call | flops 16000000000 | bytes 50000000 | tf_op jit(solution)/shard_map/tail/pallas_call | solution.py:1172
  357.7 1.3 slice.36
  359.0 0.9 reshape.67
  359.9 1.1 slice.37
  361.1 0.9 reshape.69
  363.2 1.1 slice.39
  364.3 2.0 slice.38
  366.3 0.9 copy-done.1
  367.2 4.6 %convert_element_type.17 = f32[8,384,768]{2,1,0:T(8,128)} convert(bf16[8,384,768]{2,1,0:T(8,128)(2,1)S(1)} %copy-done.1) | non-fusion elementwise | flops 2359296 | bytes 14155776 | tf_op jit(solution)/shard_map/convert_element_type | solution.py:1407
  371.8 4.4 %convert_element_type.18 = f32[8,768,384]{2,1,0:T(8,128)} convert(bf16[8,768,384]{2,1,0:T(8,128)(2,1)S(1)} %bitcast.16) | non-fusion elementwise | flops 2359296 | bytes 14155776 | tf_op jit(solution)/shard_map/convert_element_type | solution.py:1408
  (17 shorter events, 3.1 us)
Async XLA Ops:
  357.7 4.3 %copy-start.2 = (f32[16,384]{1,0:T(8,128)S(1)}, f32[16,384]{1,0:T(8,128)}, u32[]{:S(2)}) copy-start(f32[16,384]{1,0:T(8,128)} %get-tuple-element.55) | copy-start | bytes 73732
  357.7 5.5 %copy-start = (bf16[384,3072]{1,0:T(8,128)(2,1)S(1)}, bf16[384,3072]{1,0:T(8,128)(2,1)}, u32[]{:S(2)}) copy-start(bf16[384,3072]{1,0:T(8,128)(2,1)} %get-tuple-element.56) | copy-start | bytes 7077892
  363.2 4.0 %copy-start.1 = (bf16[8,384,768]{2,1,0:T(8,128)(2,1)S(1)}, bf16[8,384,768]{2,1,0:T(8,128)(2,1)}, u32[]{:S(2)}) copy-start(bf16[8,384,768]{2,1,0:T(8,128)(2,1)} %get-tuple-element.57) | copy-start | bytes 14155780
  364.3 7.5 %slice-start = ((s8[4718592]{0:T(1024)(128)(4,1)}), s8[4194304]{0:T(1024)(128)(4,1)S(1)}, s32[]{:S(2)}) async-start(s8[4718592]{0:T(1024)(128)(4,1)} %bitcast.15), calls=%async_computation | async-start | bytes 8388608
  367.2 4.6 %slice-start.1 = ((s8[4718592]{0:T(1024)(128)(4,1)}), s8[524288]{0:T(1024)(128)(4,1)S(1)}, s32[]{:S(2)}) async-start(s8[4718592]{0:T(1024)(128)(4,1)} %bitcast.15), calls=%async_computation.1 | async-start | bytes 1048576
where the time goes:
time: 384 us; the launch traced here: 377 us
  Pallas kernels  345 us (90%)
  local copies, waits for them, and re-layouts  20.7 us (5%)
  other arithmetic  9.55 us (2%)
    pallas_call x1, Pallas kernels, tail(): pl.pallas_call(tail_kernel, out_shape=(shape((rows, width), BF), shape((r...  161 us
    pallas_call x1, Pallas kernels, expert_pass(): pl.pallas_call(expert_kernel, out_shape=(shape((blocks, length, width), B...  93.9 us
    pallas_call x1, Pallas kernels, head(): pl.pallas_call(head_kernel, out_shape=(shape((2, TALL, depth), BF), shape...  90 us

commit v1 on v0

--- a/solution.py
+++ b/solution.py
@@ -452,8 +452,7 @@
     pair, shard = place_ref[0], place_ref[1]
     experts = 2 * count
 
-    def loads(expert):
-        slot = expert % 2
+    def loads(expert, slot):
         mine = pl.ds(pl.multiple_of(shard * depth, LANES), depth)
         other = pl.ds(pl.multiple_of((1 - shard) * depth, LANES), depth)
         index = pair * count + expert
@@ -464,22 +463,19 @@
             pltpu.make_async_copy(got_out.at[expert], outer.at[slot, :, other], load_sem.at[slot, 3]),
         )
 
-    def stores(expert):
-        slot = expert % 2
+    def stores(expert, slot):
         return (
             pltpu.make_async_copy(stage_in.at[slot], grad_in.at[expert], store_sem.at[slot, 0]),
             pltpu.make_async_copy(stage_out.at[slot], grad_out.at[expert], store_sem.at[slot, 1]),
         )
 
-    def fetches(block):
-        slot = block % 2
+    def fetches(block, slot):
         return (
             pltpu.make_async_copy(rows_all.at[block], rows_buf.at[slot], fetch_sem.at[slot, 0]),
             pltpu.make_async_copy(cot_all.at[block], cot_buf.at[slot], fetch_sem.at[slot, 1]),
         )
 
-    def puts(block):
-        slot = block % 2
+    def puts(block, slot):
         return (
             pltpu.make_async_copy(total_buf.at[slot], total_all.at[block], put_sem.at[slot, 0]),
             pltpu.make_async_copy(back_buf.at[slot], back_all.at[block], put_sem.at[slot, 1]),
@@ -498,7 +494,7 @@
         start(copies)
         wait(copies)
 
-    start(fetches(0) + fetches(1) + loads(0))
+    start(fetches(0, 0) + fetches(1, 1) + loads(0, 0))
     ahead = lax.broadcasted_iota(jnp.int32, (length, length), 0)
     behind = lax.broadcasted_iota(jnp.int32, (length, length), 1)
     order = jnp.where(behind < ahead, 1.0, jnp.where(behind == ahead, FAR, 0.0)).astype(BF)
@@ -508,137 +504,147 @@
     def line(expert):
         return pl.ds(experts + pair * count + expert, 1)
 
-    passes = []
-    for expert in range(count):
+    def passes_of(expert):
         highest = ranks[0, line(expert), :]
         for block in range(1, blocks):
             highest = jnp.maximum(highest, ranks[block, line(expert), :])
-        passes.append((jnp.maximum(jnp.max(highest), -1.0).astype(jnp.int32) + TILE) // TILE)
-    rounds = jnp.int32(1)
-    for value in passes:
-        rounds = jnp.maximum(rounds, value)
-
-    def one_round(step, carry):
-        again = step > 0
+        return (jnp.maximum(jnp.max(highest), -1.0).astype(jnp.int32) + TILE) // TILE
+
+    highest = ranks[0, line(0), :]
+    for block in range(blocks):
+        for expert in range(count):
+            highest = jnp.maximum(highest, ranks[block, line(expert), :])
+    rounds = (jnp.maximum(jnp.max(highest), 0.0).astype(jnp.int32) + TILE) // TILE
+
+    def take(block, slot, step):
+        at = pl.ds(pl.multiple_of(block * TILE, TILE), TILE)
+        choose = choices(block, step)
+        columns = jnp.where(lane == wanted, contract_cols(choose, flag_ref[block]), 0.0)
+        column = jnp.broadcast_to(jnp.sum(columns, -1, keepdims=True), (count * TILE, LANES))
+        wait(fetches(block, slot))
+        both = dot(choose, rows_buf[slot]).astype(BF)
+        other = dot(choose, cot_buf[slot]).astype(BF)
+        for expert in range(count):
+            part = slice(expert * TILE, (expert + 1) * TILE)
+            picked[expert, at, :] = both[part]
+            grads[expert, at, :] = other[part]
+            gate[expert, at, :] = column[part]
+
+    def compute(expert, slot):
+        def chunk(index, carry):
+            at = pl.ds(pl.multiple_of(index * CHUNK, CHUNK), CHUNK)
+            value = dot(picked[expert, at, :], inner[slot])
+            grad_active = contract_cols(grads[expert, at, :], outer[slot])
+            gate_column = gate[expert, at, 0:1]
+            square = value * value
+            bent = jnp.tanh(ROOT * value * (1.0 + CUBIC * square))
+            plus = 0.5 * (1.0 + bent)
+            bowed = value * plus
+            slope = plus + (0.5 * ROOT) * value * (1.0 - bent * bent) * (1.0 + (3.0 * CUBIC) * square)
+            active[at, :] = (bowed * gate_column).astype(BF)
+            back = (grad_active * gate_column * slope).astype(BF)
+            hidden_grad[at, :] = back
+            lane = lax.broadcasted_iota(jnp.int32, (CHUNK, TALL), 1)
+            gate_grad = jnp.sum(grad_active * bowed, -1, keepdims=True)
+            made_gate[expert, at, :] = jnp.where(lane == pair * count + expert, gate_grad, 0.0).astype(BF)
+            made[expert, at, :] = dot(active[at, :], outer[slot]).astype(BF)
+            made_back[expert, at, :] = contract_cols(back, inner[slot]).astype(BF)
+            return carry
+
+        lax.fori_loop(0, blocks * TILE // CHUNK, chunk, 0)
+
+    def weigh(expert, slot, again):
+        for stage, grad, left, right in (
+            (stage_out, grad_out, active, grads.at[expert]), (stage_in, grad_in, picked.at[expert], hidden_grad),
+        ):
+            if again:
+                reload([(grad.at[expert], stage.at[slot])])
+            for begin in range(0, left.shape[1], CHUNK):
+                at = pl.ds(begin, CHUNK)
+                value = contract_rows(left[:, at], right[...])
+                if again:
+                    value = value + stage[slot, at, :].astype(F32)
+                stage[slot, at, :] = value.astype(BF)
+
+    def give(block, slot, step, again):
+        at = pl.ds(pl.multiple_of(block * TILE, TILE), TILE)
+        choose = choices(block, step)
+
+        def joined(source):
+            return jnp.concatenate([source[expert, at, :] for expert in range(count)], 0)
+
+        if again:
+            reload([(total_all.at[block], rows_buf.at[0]), (back_all.at[block], rows_buf.at[1])])
+        for target, source, old in ((total_buf, made, 0), (back_buf, made_back, 1)):
+            value = contract_rows(choose, joined(source))
+            if again:
+                value = value + rows_buf[old].astype(F32)
+            target[slot] = value.astype(BF)
+        start(puts(block, slot))
+        gates = contract_rows(joined(made_gate), choose)
+        if again:
+            gates = gates + gate_ref[block].astype(F32)
+        gate_ref[block] = gates.astype(BF)
+
+    def choices(block, step):
         slots = lax.broadcasted_iota(jnp.int32, (TILE, length), 0).astype(F32) + (step * TILE).astype(F32)
-
-        def choices(block):
-            return jnp.concatenate(
-                [(ranks[block, line(expert), :] == slots).astype(BF) for expert in range(count)], 0
-            )
-
-        @pl.when(again)
-        def _():
-            start(fetches(0) + fetches(1) + loads(0))
-
-        lane = lax.broadcasted_iota(jnp.int32, (count * TILE, TALL), 1)
-        wanted = lax.broadcasted_iota(jnp.int32, (count * TILE, TALL), 0) // TILE + pair * count
-        for block in range(blocks):
-            slot = block % 2
-            at = pl.ds(block * TILE, TILE)
-            choose = choices(block)
-            columns = jnp.where(lane == wanted, contract_cols(choose, flag_ref[block]), 0.0)
-            column = jnp.broadcast_to(jnp.sum(columns, -1, keepdims=True), (count * TILE, LANES))
-            wait(fetches(block))
-            both = dot(choose, rows_buf[slot]).astype(BF)
-            other = dot(choose, cot_buf[slot]).astype(BF)
-            for expert in range(count):
-                part = slice(expert * TILE, (expert + 1) * TILE)
-                picked[expert, at, :] = both[part]
-                grads[expert, at, :] = other[part]
-                gate[expert, at, :] = column[part]
-            if block + 2 < blocks:
-                start(fetches(block + 2))
-
-        for expert in range(count):
-            slot = expert % 2
-            runs = jnp.logical_or(step == 0, passes[expert] > step)
-            if expert + 1 < count:
-                start(loads(expert + 1))
-            wait(loads(expert))
-
-            @pl.when(runs)
+        return jnp.concatenate([(ranks[block, line(expert), :] == slots).astype(BF) for expert in range(count)], 0)
+
+    lane = lax.broadcasted_iota(jnp.int32, (count * TILE, TALL), 1)
+    wanted = lax.broadcasted_iota(jnp.int32, (count * TILE, TALL), 0) // TILE + pair * count
+    first = jnp.int32(0)
+    for block in range(blocks):
+        take(block, block % 2, first)
+        if block + 2 < blocks:
+            start(fetches(block + 2, block % 2))
+    for expert in range(count):
+        slot = expert % 2
+        if expert + 1 < count:
+            start(loads(expert + 1, 1 - slot))
+        wait(loads(expert, slot))
+        compute(expert, slot)
+        if expert >= 2:
+            wait(stores(expert - 2, slot))
+        weigh(expert, slot, False)
+        start(stores(expert, slot))
+    for block in range(blocks):
+        if block >= 2:
+            wait(puts(block - 2, block % 2))
+        give(block, block % 2, first, False)
+    for block in range(blocks - 2, blocks):
+        wait(puts(block, block % 2))
+    for expert in range(count - 2, count):
+        wait(stores(expert, expert % 2))
+
+    def more(step, carry):
+        def take_one(block, carry):
+            start(fetches(block, 0))
+            take(block, 0, step)
+            return carry
+
+        def expert_one(expert, carry):
+            @pl.when(passes_of(expert) > step)
             def _():
-                def chunk(index, carry):
-                    at = pl.ds(pl.multiple_of(index * CHUNK, CHUNK), CHUNK)
-                    value = dot(picked[expert, at, :], inner[slot])
-                    grad_active = contract_cols(grads[expert, at, :], outer[slot])
-                    gate_column = gate[expert, at, 0:1]
-                    square = value * value
-                    bent = jnp.tanh(ROOT * value * (1.0 + CUBIC * square))
-                    plus = 0.5 * (1.0 + bent)
-                    bowed = value * plus
-                    slope = plus + (0.5 * ROOT) * value * (1.0 - bent * bent) * (1.0 + (3.0 * CUBIC) * square)
-                    active[at, :] = (bowed * gate_column).astype(BF)
-                    back = (grad_active * gate_column * slope).astype(BF)
-                    hidden_grad[at, :] = back
-                    lane = lax.broadcasted_iota(jnp.int32, (CHUNK, TALL), 1)
-                    gate_grad = jnp.sum(grad_active * bowed, -1, keepdims=True)
-                    made_gate[expert, at, :] = jnp.where(lane == pair * count + expert, gate_grad, 0.0).astype(BF)
-                    made[expert, at, :] = dot(active[at, :], outer[slot]).astype(BF)
-                    made_back[expert, at, :] = contract_cols(back, inner[slot]).astype(BF)
-                    return carry
-
-                lax.fori_loop(0, blocks * TILE // CHUNK, chunk, 0)
-
-            if expert >= 2:
-                before = jnp.logical_or(step == 0, passes[expert - 2] > step)
-
-                @pl.when(before)
-                def _():
-                    wait(stores(expert - 2))
-
-            @pl.when(runs)
-            def _():
-                for stage, grad, left, right in (
-                    (stage_out, grad_out, active, grads.at[expert]), (stage_in, grad_in, picked.at[expert], hidden_grad),
-                ):
-                    @pl.when(again)
-                    def _():
-                        reload([(grad.at[expert], stage.at[slot])])
-
-                    for begin in range(0, left.shape[1], CHUNK):
-                        at = pl.ds(begin, CHUNK)
-                        value = contract_rows(left[:, at], right[...])
-                        old = stage[slot, at, :].astype(F32)
-                        stage[slot, at, :] = (value + jnp.where(again, old, 0.0)).astype(BF)
-                start(stores(expert))
-
-        for block in range(blocks):
-            slot = block % 2
-            at = pl.ds(block * TILE, TILE)
-            choose = choices(block)
-            if block >= 2:
-                wait(puts(block - 2))
-
-            def joined(source):
-                return jnp.concatenate([source[expert, at, :] for expert in range(count)], 0)
-
-            @pl.when(again)
-            def _():
-                reload([(total_all.at[block], rows_buf.at[0]), (back_all.at[block], rows_buf.at[1])])
-
-            for target, source, old in ((total_buf, made, 0), (back_buf, made_back, 1)):
-                target[slot] = contract_rows(choose, joined(source)).astype(BF)
-
-                @pl.when(again)
-                def _():
-                    target[slot] = (target[slot].astype(F32) + rows_buf[old].astype(F32)).astype(BF)
-
-            start(puts(block))
-            gates = contract_rows(joined(made_gate), choose)
-            gate_ref[block] = (gates + jnp.where(again, gate_ref[block].astype(F32), 0.0)).astype(BF)
-        for block in range(blocks - 2, blocks):
-            wait(puts(block))
-        for expert in range(count - 2, count):
-
-            @pl.when(jnp.logical_or(step == 0, passes[expert] > step))
-            def _():
-                wait(stores(expert))
-
+                start(loads(expert, 0))
+                wait(loads(expert, 0))
+                compute(expert, 0)
+                weigh(expert, 0, True)
+                start(stores(expert, 0))
+                wait(stores(expert, 0))
+
+            return carry
+
+        def give_one(block, carry):
+            give(block, 0, step, True)
+            wait(puts(block, 0))
+            return carry
+
+        lax.fori_loop(0, blocks, take_one, 0)
+        lax.fori_loop(0, count, expert_one, 0)
+        lax.fori_loop(0, blocks, give_one, 0)
         return carry
 
-    lax.fori_loop(0, rounds, one_round, 0)
+    lax.fori_loop(1, rounds, more, 0)
 
 
 def expert_pass(place, rows, flags, cot, own_in, got_in, own_out, got_out):

time: 384 us -> 357 us (0.930)
  Pallas kernels: 345 us -> 321 us
    pallas_call x1, Pallas kernels: 93.9 us -> 69.8 us  [expert_pass(): pl.pallas_call(expert_kernel, out_shape=(shape((blocks, length, width), B...]
where the time goes in v1:
time: 357 us; the launch traced here: 352 us
  Pallas kernels  321 us (90%)
  local copies, waits for them, and re-layouts  20.7 us (6%)
  other arithmetic  9.55 us (3%)
    pallas_call x1, Pallas kernels, tail(): pl.pallas_call(tail_kernel, out_shape=(shape((rows, width), BF), shape((r...  161 us
    pallas_call x1, Pallas kernels, head(): pl.pallas_call(head_kernel, out_shape=(shape((2, TALL, depth), BF), shape...  90 us
    pallas_call x1, Pallas kernels, expert_pass(): pl.pallas_call(expert_kernel, out_shape=(shape((blocks, length, width), B...  69.8 us

profile of v1, /device:TPU:17, one launch (start us, length us, event | category | flops | bytes accessed | tf_op | source)
XLA Modules:
  0.0 352.5 jit_solution(17626340842010002875)
XLA Ops:
  1.2 0.7 broadcast_in_dim.12
  1.9 0.7 broadcast_in_dim.13
  2.6 0.7 broadcast_in_dim.14
  4.0 0.8 reshape.64
  4.7 0.7 concatenate.3
  6.1 0.7 reshape.65.ids_ref
  6.8 0.8 reshape.62
  7.6 0.7 reshape.63.noise_ref
  8.3 1.2 reshape.58
  9.5 0.9 pad.19
  10.4 1.2 reshape.60
  11.6 0.9 pad.20
  12.4 90.0 %head.1 = (bf16[2,16,384]{2,1,0:T(8,128)(2,1)}, bf16[768,2304]{1,0:T(8,128)(2,1)}, bf16[768,768]{1,0:T(8,128)(2,1)}, bf16[416,768]{1,0:T(8,128)(2,1)}, bf16[416,...) custom-call(bf16[416,768]{1,0:T(8,128)(2,1)} %bitcast.17, ...), custom_call_target="tpu_custom_call" | custom-call | flops 8000000000 | bytes 30000000 | tf_op jit(solution)/shard_map/head/pallas_call | solution.py:411
  102.5 69.8 %experts.1 = (bf16[8,416,768]{2,1,0:T(8,128)(2,1)}, bf16[8,416,768]{2,1,0:T(8,128)(2,1)}, bf16[8,16,416]{2,1,0:T(8,128)(2,1)}, bf16[4,768,768]{2,1,0:T(8,128)(2,1)}, bf16[4,768,768]{2,1,0:T(8,128)(2,1)}) custom-call(s32[2]{0:T(128)} %pad_add_fusion.place_ref, bf16[8,16,416]{2,1,0:T(8,128)(2,1)} %get-tuple-element.35.flag_ref.flags_all, ...), custom_call_target="tpu_custom_call" | custom-call | flops 49999998976 | bytes 50000000 | tf_op jit(solution)/shard_map/experts/pallas_call | solution.py:657
  172.3 161.4 %tail.1 = (bf16[416,768]{1,0:T(8,128)(2,1)}, bf16[416,768]{1,0:T(8,128)(2,1)}, bf16[384,3072]{1,0:T(8,128)(2,1)}, f32[16,384]{1,0:T(8,128)}, bf16[8,384,768]{2,1...) custom-call(bf16[8,416,768]{2,1,0:T(8,128)(2,1)} %get-tuple-element.40.ba, ...), custom_call_target="tpu_custom_call" | custom-call | flops 16000000000 | bytes 50000000 | tf_op jit(solution)/shard_map/tail/pallas_call | solution.py:1178
  333.8 1.3 slice.36
  335.0 0.9 reshape.67
  336.0 1.1 slice.37
  337.1 0.9 reshape.69
  339.3 1.1 slice.39
  340.3 2.0 slice.38
  342.4 0.9 copy-done.1
  343.3 4.6 %convert_element_type.17 = f32[8,384,768]{2,1,0:T(8,128)} convert(bf16[8,384,768]{2,1,0:T(8,128)(2,1)S(1)} %copy-done.1) | non-fusion elementwise | flops 2359296 | bytes 14155776 | tf_op jit(solution)/shard_map/convert_element_type | solution.py:1413
  347.9 4.4 %convert_element_type.18 = f32[8,768,384]{2,1,0:T(8,128)} convert(bf16[8,768,384]{2,1,0:T(8,128)(2,1)S(1)} %bitcast.16) | non-fusion elementwise | flops 2359296 | bytes 14155776 | tf_op jit(solution)/shard_map/convert_element_type | solution.py:1414
  (17 shorter events, 3.1 us)
Async XLA Ops:
  333.7 4.3 %copy-start.2 = (f32[16,384]{1,0:T(8,128)S(1)}, f32[16,384]{1,0:T(8,128)}, u32[]{:S(2)}) copy-start(f32[16,384]{1,0:T(8,128)} %get-tuple-element.55) | copy-start | bytes 73732
  333.7 5.5 %copy-start = (bf16[384,3072]{1,0:T(8,128)(2,1)S(1)}, bf16[384,3072]{1,0:T(8,128)(2,1)}, u32[]{:S(2)}) copy-start(bf16[384,3072]{1,0:T(8,128)(2,1)} %get-tuple-element.56) | copy-start | bytes 7077892
  339.2 4.0 %copy-start.1 = (bf16[8,384,768]{2,1,0:T(8,128)(2,1)S(1)}, bf16[8,384,768]{2,1,0:T(8,128)(2,1)}, u32[]{:S(2)}) copy-start(bf16[8,384,768]{2,1,0:T(8,128)(2,1)} %get-tuple-element.57) | copy-start | bytes 14155780
  340.3 7.5 %slice-start = ((s8[4718592]{0:T(1024)(128)(4,1)}), s8[4194304]{0:T(1024)(128)(4,1)S(1)}, s32[]{:S(2)}) async-start(s8[4718592]{0:T(1024)(128)(4,1)} %bitcast.15), calls=%async_computation | async-start | bytes 8388608
  343.3 4.6 %slice-start.1 = ((s8[4718592]{0:T(1024)(128)(4,1)}), s8[524288]{0:T(1024)(128)(4,1)S(1)}, s32[]{:S(2)}) async-start(s8[4718592]{0:T(1024)(128)(4,1)} %bitcast.15), calls=%async_computation.1 | async-start | bytes 1048576

commit v2 on v1

--- a/solution.py
+++ b/solution.py
@@ -247,12 +247,21 @@
         )
 
 
+def pad_images(source, target):
+    value = source[...].astype(F32)
+    empty = jnp.zeros((PAD - SEQ, value.shape[1]), F32)
+    for image in range(2):
+        part = value[image * SEQ : (image + 1) * SEQ]
+        target[pl.ds(image * PAD, PAD), :] = jnp.concatenate((part, empty), 0).astype(BF)
+
+
 def head_kernel(
-    x_ref, cot_ref, small_own, qkv_own, out_own, expert_in, expert_out, noise_ref, ids_ref,
+    tokens_own, cot_own, small_own, qkv_own, out_own, expert_in, expert_out, noise_ref, ids_ref,
     small_ref, qkv_ref, out_ref, normed_ref, packed_ref, attended_ref, middle_ref, prob_ref,
-    rows_all, flags_all, cot_all, got_in, got_out,
+    x_ref, cot_ref, rows_all, flags_all, cot_all, got_in, got_out,
     sent_rows, sent_flags, send, recv, local_sem,
 ):
+    pad_images(cot_own, cot_ref)
     place = Place()
     links = Links(send, recv)
     width = x_ref.shape[1]
@@ -298,6 +307,8 @@
     cot_line = LineGather(links, place, slots(cot_all), lambda part: cot_ref.at[pl.ds(part * PAD, PAD), :], 2)
     for part in range(2):
         cot_line.start(part, 0)
+
+    pad_images(tokens_own, x_ref)
 
     beside, twins = [], []
     for index, (own, full, start, size) in enumerate(pieces):
@@ -402,7 +413,7 @@
 
 
 def head(x, cot, small, qkv, out, expert_in, expert_out, noise, ids):
-    rows, width = x.shape
+    rows, width = x.shape[0] // SEQ * PAD, x.shape[1]
     depth = qkv.shape[0]
     count = expert_in.shape[0] // 2
     shape = jax.ShapeDtypeStruct
@@ -419,6 +430,8 @@
             shape((rows, width), BF),
             shape((rows, width), F32),
             shape((TALL, rows), F32),
+            shape((rows, width), BF),
+            shape((rows, width), BF),
             shape((8, rows, width), BF),
             shape((8, TALL, rows), BF),
             shape((8, rows, width), BF),
@@ -426,7 +439,7 @@
             shape((count,) + expert_out.shape[1:], BF),
         ),
         in_specs=[vmem] * 3 + [anywhere] * 4 + [vmem] * 2,
-        out_specs=(vmem,) * 8 + (anywhere,) * 5,
+        out_specs=(vmem,) * 10 + (anywhere,) * 5,
         scratch_shapes=[
             pltpu.VMEM((rows, width), BF),
             pltpu.VMEM((TALL, rows), BF),
@@ -712,7 +725,19 @@
     return cot + norm_back(grad, unit, inverse, gain_row(small_ref, experts, 2))
 
 
-def back_heads(at, double, grad_proj, packed_ref, out_ref, stacked):
+def back_probs(at, double, packed_ref, take):
+    group = 3 * HEAD_DIM
+    scale = HEAD_DIM ** (-0.5)
+    lanes = lax.broadcasted_iota(jnp.int32, (PAD, group), 1) // HEAD_DIM
+    packed = packed_ref[at, pl.ds(double * 6 * group, 6 * group)]
+    for side in range(2):
+        query, keys = (packed[:, (3 * side + k) * group : (3 * side + k + 1) * group] for k in range(2))
+        for head in range(3):
+            masked = jnp.where(lanes == head, query, jnp.zeros_like(query))
+            take(side * 3 + head, head_probs(masked, keys, scale))
+
+
+def back_heads(at, double, grad_proj, packed_ref, out_ref, stacked, give):
     width = grad_proj.shape[1]
     group = 3 * HEAD_DIM
     scale = HEAD_DIM ** (-0.5)
@@ -726,14 +751,15 @@
         outs = [jnp.zeros((PAD, group), F32) for _ in range(3)]
         for head in range(3):
             mask = lanes == head
-            probs = head_probs(jnp.where(mask, query, jnp.zeros_like(query)), keys, scale)
+            low = give(side * 3 + head)
+            probs = low.astype(F32)
             part = jnp.where(mask, grad_att, jnp.zeros_like(grad_att))
             grad_weights = contract_cols(part, values)
             inner_sum = jnp.sum(probs * grad_weights, -1, keepdims=True)
             grad_scores = (probs * (grad_weights - inner_sum)).astype(BF)
             outs[0] = jnp.where(mask, dot(grad_scores, keys), outs[0])
             outs[1] = jnp.where(mask, contract_rows(grad_scores, query), outs[1])
-            outs[2] = jnp.where(mask, contract_rows(probs.astype(BF), grad_att), outs[2])
+            outs[2] = jnp.where(mask, contract_rows(low, grad_att), outs[2])
         made += [outs[0] * scale, outs[1] * scale, outs[2]]
     stacked[at, pl.ds(double * 6 * group, 6 * group)] = jnp.concatenate(made, 1).astype(BF)
 
@@ -757,7 +783,9 @@
         grad_proj = grad_middle.astype(BF)
         projected[at, :] = grad_proj
         for double in range(width // (6 * HEAD_DIM)):
-            back_heads(at, double, grad_proj, packed_ref, out_ref, stacked)
+            saved = {}
+            back_probs(at, double, packed_ref, lambda index, value: saved.update({index: value.astype(BF)}))
+            back_heads(at, double, grad_proj, packed_ref, out_ref, stacked, saved.get)
         grad = contract_cols(stacked[at, :], qkv_ref[...])
         unit, inverse = norm_parts(x_ref[at, :].astype(F32))
         sums[0] = sums[0] + jnp.sum(grad * unit, 0, keepdims=True)
@@ -788,7 +816,7 @@
     )(moe, gates, cot, x, middle, sent, flags, prob, attended, packed, normed, small, qkv, out)
 
 
-ORDER = [[('x', 0), ('x', 1)], [('x', 2)], [('a', 0), ('x', 3), ('a', 1), ('x', 4), ('y', 0), ('x', 5)], [], [], [], [], [('b', 0), ('x', 6)], [('da', 0), ('b', 1), ('y', 1), ('da', 2), ('da', 3), ('y', 2), ('dl', 0), ('da', 1), ('x', 7)], [('dl', 2), ('y', 3), ('x', 8), ('dl', 3), ('db', 0), ('x', 9), ('y', 4), ('db', 2), ('y', 5), ('y', 6), ('dl', 1), ('y', 7), ('ds', 0), ('db', 3), ('c', 0), ('y', 8), ('s', 0), ('x', 10), ('c', 1), ('ds', 2), ('y', 9), ('s', 1), ('y', 10), ('s', 2), ('db', 1), ('ds', 3), ('dt', 0), ('ds', 1), ('dt', 2), ('x', 11), ('y', 11)], [('s', 3), ('dt', 3), ('dt', 1)]]
+ORDER = [[('x', 0), ('n', 3)], [('a', 0), ('x', 1), ('n', 4)], [], [('b', 0), ('n', 5), ('x', 2), ('y', 0), ('y', 1)], [('n', 6), ('a', 1)], [('x', 3), ('c', 0)], [('da', 1), ('x', 4)], [('x', 5), ('da', 0), ('n', 7), ('dl', 1), ('y', 2), ('x', 6)], [('dl', 0)], [('da', 3), ('db', 1), ('x', 7), ('n', 8), ('db', 0), ('n', 9), ('da', 2), ('dl', 3), ('y', 3), ('n', 10), ('b', 1), ('ds', 1), ('ds', 0), ('x', 8)], [('y', 4), ('c', 1), ('y', 5), ('x', 9), ('dl', 2), ('s', 0), ('db', 3), ('n', 11), ('y', 6), ('d1', 0), ('y', 7), ('ds', 3), ('s', 1), ('db', 2), ('x', 10), ('y', 8)], [('d2', 0), ('ds', 2), ('d1', 1), ('x', 11), ('dt', 3), ('s', 2), ('d1', 2), ('d2', 1), ('y', 9), ('dt', 0), ('y', 10), ('d2', 2), ('y', 11), ('s', 3), ('dt', 1), ('dt', 2)]]
 
 
 class LineScatter:
@@ -837,7 +865,7 @@
     cot_ref, x_ref, middle_ref, prob_ref, attended_ref, packed_ref, normed_ref, small_ref, qkv_ref, out_ref,
     mixed_ref, tokens_ref, dense_ref, grad_small, final_in, final_out, beside_in, beside_out,
     back_sum, back_got, back_up, back_down, gate_sum, gate_got, gate_up, gate_down,
-    total_sum, total_got, total_up, total_down, moe, gates, rows_ref, flag_ref, projected, stacked,
+    total_sum, total_got, total_up, total_down, moe, gates, rows_ref, flag_ref, projected, stacked, weights_ref,
     chunks, core_got, across_sent, across_got, line_sum, line_got, side_sum, side_got, line_final,
     own_in, own_out, across_in, across_out, read_in, read_out, half_in, half_out, mine_in, mine_out, both_in, both_out,
     small_sent, small_core, small_half, small_across, small_side, small_beside, small_line_sent, small_line,
@@ -910,7 +938,6 @@
 
     def take_across(m):
         at_across[m].wait_recv()
-        send_across()
         loads[m].wait()
         add(pieces[m][2], pieces[m][5])
         at_beside[m] = links.start(pieces[m][2], pieces[m][3], place.beside)
@@ -1009,13 +1036,31 @@
         target = dense_ref.at[
             pl.ds(pl.multiple_of(pair * share + tensor * piece, TALL), piece), pl.ds(k * width, width)
         ]
-        stage["spread", k] = [links.start(line_final.at[k], target, around(offset)) for offset in (2, 1, 3)]
         stage["keep", k] = pltpu.make_async_copy(line_final.at[k], target, local_sem.at[24 + k])
         stage["keep", k].start()
+        if k < 3:
+            dense_line_back.start(k, 0)
+        else:
+            stage["spread", k] = [links.start(line_final.at[k], target, around(offset)) for offset in (2, 1, 3)]
+
+    def dense_hop(k, step):
+        dense_line_back.wait(k, step)
+        dense_line_back.start(k, step + 1)
+
+    dense_line_back = LineGather(
+        links, place,
+        lambda slot, k: dense_ref.at[
+            pl.ds(pl.multiple_of(pair * share + slot * piece, TALL), piece), pl.ds(k * width, width)
+        ],
+        lambda k: line_final.at[k], 3,
+    )
 
     def dense_twin(k):
-        for copy in stage["spread", k]:
-            copy.wait_recv()
+        if k < 3:
+            dense_line_back.wait(k, 2)
+        else:
+            for copy in stage["spread", k]:
+                copy.wait_recv()
         stage["keep", k].wait()
         block = dense_ref.at[pl.ds(pl.multiple_of(pair * share, TALL), share), pl.ds(k * width, width)]
         stage["twin", k] = links.start(block, block, place.twin)
@@ -1058,7 +1103,8 @@
     )
 
     steps = {
-        "x": take_across, "y": take_beside, "a": first_sum, "b": first_total, "c": first_share,
+        "d1": lambda index: dense_hop(index, 0), "d2": lambda index: dense_hop(index, 1),
+        "n": lambda index: send_across(), "x": take_across, "y": take_beside, "a": first_sum, "b": first_total, "c": first_share,
         "da": dense_across, "dl": dense_line, "db": dense_beside, "ds": dense_spread, "dt": dense_twin,
         "s": lambda index: (small_core_stage, small_across_stage, small_beside_stage, small_line_stage)[index](),
     }
@@ -1066,6 +1112,32 @@
     def go(slot):
         for name, index in ORDER[slot]:
             steps[name](index)
+
+    def save_probs(double, image):
+        at = pl.ds(image * PAD, PAD)
+
+        def take(index, value):
+            weights_ref[(image * 2 + double) * 6 + index] = value.astype(BF)
+
+        back_probs(at, double, packed_ref, take)
+
+    def use_heads(double, image):
+        at = pl.ds(image * PAD, PAD)
+        back_heads(
+            at, double, projected[at, :], packed_ref, out_ref, stacked,
+            lambda index: weights_ref[(image * 2 + double) * 6 + index],
+        )
+
+    def middle_of(image):
+        at = pl.ds(image * PAD, PAD)
+        cols = slice(image * PAD, (image + 1) * PAD)
+        back_line.finish(image, moe.at[at, :])
+        grad = back_middle(
+            at, moe[at, :], gates[:, cols], cot_ref[at, :].astype(F32), middle_ref[at, :], rows_ref[at, :],
+            prob_ref[:, cols], flag_ref[:, cols].astype(F32), small_ref, sums,
+        )
+        moe[at, :] = grad
+        projected[at, :] = grad.astype(BF)
 
     first_send(0)
     for _ in range(3):
@@ -1088,74 +1160,69 @@
     from_twin[3].wait_recv()
     for slot in range(4):
         add(total_sum.at[slot], total_got.at[slot])
+    save_probs(0, 0)
     go(0)
     gate_line.send(0, 1)
-    for part in range(2):
-        back_line.send(part, 1)
+    back_line.send(0, 1)
+    save_probs(0, 1)
+    back_line.send(1, 1)
     go(1)
+    save_probs(1, 0)
     gate_line.send(0, 2)
-    for part in range(2):
-        back_line.send(part, 2)
+    back_line.send(0, 2)
     go(2)
+    back_line.send(1, 2)
+    save_probs(1, 1)
+    go(3)
     for part in range(2):
         total_line.send(part, 0)
     gate_line.finish(0, gates)
     locals_[3].wait()
     locals_[4].wait()
-
     sums = [jnp.zeros((1, width), F32) for _ in range(4)] + [jnp.zeros((TALL, width), F32)]
-    for image in range(2):
-        at = pl.ds(image * PAD, PAD)
-        cols = slice(image * PAD, (image + 1) * PAD)
-        back_line.finish(image, moe.at[at, :])
-        grad = back_middle(
-            at, moe[at, :], gates[:, cols], cot_ref[at, :].astype(F32), middle_ref[at, :], rows_ref[at, :],
-            prob_ref[:, cols], flag_ref[:, cols].astype(F32), small_ref, sums,
-        )
-        moe[at, :] = grad
-        projected[at, :] = grad.astype(BF)
-    go(3)
+    middle_of(0)
+    use_heads(0, 0)
+    go(4)
+    middle_of(1)
     chunks[0] = contract_rows(attended_ref[...], projected[...]).astype(BF)
     dense_core(0)
-    go(4)
-    for image in range(2):
-        at = pl.ds(image * PAD, PAD)
-        back_heads(at, 0, projected[at, :], packed_ref, out_ref, stacked)
-        if image == 0:
-            go(5)
+    go(5)
+    use_heads(0, 1)
     chunks[1] = contract_rows(normed_ref[...], stacked[:, pl.ds(0, width)]).astype(BF)
     dense_core(1)
+    go(6)
     for part in range(2):
         total_line.send(part, 1)
-    go(6)
-    for image in range(2):
-        at = pl.ds(image * PAD, PAD)
-        back_heads(at, 1, projected[at, :], packed_ref, out_ref, stacked)
-        if image == 0:
-            go(7)
+    use_heads(1, 0)
+    go(7)
+    use_heads(1, 1)
     for k in (2, 3):
         chunks[k] = contract_rows(normed_ref[...], stacked[:, pl.ds((k - 1) * width, width)]).astype(BF)
         dense_core(k)
+    go(8)
     for part in range(2):
         total_line.send(part, 2)
-    go(8)
+    go(9)
+    joined = []
     for image in range(2):
         at = pl.ds(image * PAD, PAD)
         grad = contract_cols(stacked[at, :], qkv_ref[...])
         unit, inverse = norm_parts(x_ref[at, :].astype(F32))
         sums[0] = sums[0] + jnp.sum(grad * unit, 0, keepdims=True)
         sums[1] = sums[1] + jnp.sum(grad, 0, keepdims=True)
-        tokens_ref[at, :] = (
-            moe[at, :] + norm_back(grad, unit, inverse, gain_row(small_ref, experts, 0))
-        ).astype(BF)
+        grad = moe[at, :] + norm_back(grad, unit, inverse, gain_row(small_ref, experts, 0))
+        joined.append(grad[:SEQ])
+    tokens_ref[...] = jnp.concatenate(joined, 0).astype(BF)
     small_sent[...] = jnp.concatenate([sums[4][0:experts]] + sums[:4] + [jnp.zeros((4, width), F32)], 0)
     small_core_copy = links.start(small_sent, small_core, place.twin)
-    go(9)
+    go(10)
+    joined = []
     for part in range(2):
         at = pl.ds(part * PAD, PAD)
         total_line.finish(part, moe.at[at, :])
-        mixed_ref[at, :] = (middle_ref[at, :] + moe[at, :]).astype(BF)
-    go(10)
+        joined.append((middle_ref[at, :] + moe[at, :])[:SEQ])
+    mixed_ref[...] = jnp.concatenate(joined, 0).astype(BF)
+    go(11)
     for copy in at_twin + [stage["twin", k] for k in range(4)]:
         copy.wait_recv()
     for copy in kept:
@@ -1178,8 +1245,8 @@
     return pl.pallas_call(
         tail_kernel,
         out_shape=(
-            shape((rows, width), BF),
-            shape((rows, width), BF),
+            shape((rows // PAD * SEQ, width), BF),
+            shape((rows // PAD * SEQ, width), BF),
             shape((depth, 4 * width), BF),
             shape((TALL, depth), F32),
             shape((2 * count, depth, hidden), BF),
@@ -1199,6 +1266,7 @@
             pltpu.VMEM((TALL, rows), BF),
             pltpu.VMEM((rows, width), BF),
             pltpu.VMEM((rows, 3 * width), BF),
+            pltpu.VMEM((24, PAD, PAD), BF),
             pltpu.VMEM((4, width, width), BF),
             pltpu.VMEM((4, 2, share, width), BF),
             pltpu.VMEM((4, share, width), BF),
@@ -1227,7 +1295,7 @@
             pltpu.SemaphoreType.DMA((192,)),
             pltpu.SemaphoreType.DMA((48,)),
         ],
-        compiler_params=pltpu.CompilerParams(vmem_limit_bytes=BIG, collective_id=2, has_side_effects=True),
+        compiler_params=pltpu.CompilerParams(vmem_limit_bytes=BIG + 3 * 512 * 1024, collective_id=2, has_side_effects=True),
         cost_estimate=pl.CostEstimate(flops=16 * 10**9, bytes_accessed=5 * 10**7, transcendentals=10**6),
         name="tail",
     )(back_all, gate_all, total_all, grads_in, grads_out, rows_all, flags_all, cot, x, middle, prob, attended, packed, normed, small, qkv, out)
@@ -1361,20 +1429,19 @@
     def unpad(value):
         return value.reshape(images, PAD, value.shape[1])[:, :SEQ].reshape(rows, value.shape[1])
 
-    small = jnp.concatenate(
-        (router_weight.T, ln1_gain[None], ln1_bias[None], ln2_gain[None], ln2_bias[None]), 0
-    )
-    small = jnp.pad(small, ((0, TALL - small.shape[0]), (0, 0)))
-    cot, x = pad(cotangent), pad(tokens)
+    vectors = jnp.concatenate((ln1_gain, ln1_bias, ln2_gain, ln2_bias, jnp.zeros_like(jnp.tile(ln1_gain, 4))))
+    vectors = lax.optimization_barrier(vectors).reshape(8, ln1_gain.shape[0])
+    small = jnp.concatenate((router_weight.T, vectors), 0)
     noise, ids = pad_turned(route_noise, TALL, 0), pad_turned(expert_ids, 8, -1)
     place = jnp.stack((comm.pair, comm.shard if comm.sizes[0] == 2 else 0 * comm.shard)).astype(jnp.int32)
     if comm.sizes[0] == 2:
         (
             small, proj_qkv, proj_out, normed_a, packed, attended, middle, prob,
-            rows_all, flags_all, grad_rows, got_in, got_out,
-        ) = head(x, cot, small, qkv_weight, out_weight, expert_in, expert_out, noise, ids)
+            x, cot, rows_all, flags_all, grad_rows, got_in, got_out,
+        ) = head(tokens, cotangent, small, qkv_weight, out_weight, expert_in, expert_out, noise, ids)
         weights = (expert_in, got_in, expert_out, got_out)
     else:
+        cot, x = pad(cotangent), pad(tokens)
         small = lax.all_gather(small, "shard", axis=1, tiled=True)
         small = small.reshape(TALL, 2, width // 2).transpose(1, 0, 2)
         proj_qkv = lax.all_gather(qkv_weight, "shard", axis=0, tiled=True)
@@ -1401,8 +1468,8 @@
         )
         dense = dense.astype(F32)
         return (
-            unpad(mixed),
-            unpad(grad_tokens),
+            mixed,
+            grad_tokens,
             grad_small[experts],
             grad_small[experts + 1],
             dense[:, width:],

time: 357 us -> 345 us (0.966)
  Pallas kernels: 321 us -> 313 us
  local copies, waits for them, and re-layouts: 20.7 us -> 15.5 us
    pallas_call x1, Pallas kernels: 161 us -> 152 us  [tail(): pl.pallas_call(tail_kernel, out_shape=(shape((rows // PAD * SEQ, width),...]
    reshape x4 -> x1, local copies, waits for them, and re-layouts: 4.29 us -> 0.01 us  [local(): vectors = lax.optimization_barrier(vectors).reshape(8, ln1_gain.shape[0])]
    unnamed x10 -> x18, local copies, waits for them, and re-layouts: 0.91 us -> 5.1 us
where the time goes in v2:
time: 345 us; the launch traced here: 340 us
  Pallas kernels  313 us (91%)
  local copies, waits for them, and re-layouts  15.5 us (4%)
  other arithmetic  10.8 us (3%)
    pallas_call x1, Pallas kernels, tail(): pl.pallas_call(tail_kernel, out_shape=(shape((rows // PAD * SEQ, width),...  152 us
    pallas_call x1, Pallas kernels, head(): pl.pallas_call(head_kernel, out_shape=(shape((2, TALL, depth), BF), shape...  90.4 us
    pallas_call x1, Pallas kernels, expert_pass(): pl.pallas_call(expert_kernel, out_shape=(shape((blocks, length, width), B...  69.8 us

profile of v2, /device:TPU:17, one launch (start us, length us, event | category | flops | bytes accessed | tf_op | source)
XLA Modules:
  0.0 340.0 jit_solution(16562358454810140364)
XLA Ops:
  0.7 0.6 pad_add_fusion.place_ref
  1.2 0.8 reshape.40
  2.0 0.9 dynamic-update-slice
  2.9 0.9 dynamic-update-slice.1
  3.7 0.9 dynamic-update-slice.2
  4.6 0.9 dynamic-update-slice.3
  5.4 0.3 dynamic-update-slice.4
  5.7 1.3 pad_maximum_fusion.small_own
  7.0 0.7 reshape.41.ids_ref
  7.7 0.8 reshape.38
  8.5 0.7 reshape.39.noise_ref
  9.2 90.4 %head.1 = (bf16[2,16,384]{2,1,0:T(8,128)(2,1)}, bf16[768,2304]{1,0:T(8,128)(2,1)}, bf16[768,768]{1,0:T(8,128)(2,1)}, bf16[416,768]{1,0:T(8,128)(2,1)}, bf16[416,...) custom-call(bf16[394,768]{1,0:T(8,128)(2,1)} %tokens_own.1, ...), custom_call_target="tpu_custom_call" | custom-call | flops 8000000000 | bytes 30000000 | tf_op jit(solution)/shard_map/head/pallas_call | solution.py:422
  99.7 69.8 %experts.1 = (bf16[8,416,768]{2,1,0:T(8,128)(2,1)}, bf16[8,416,768]{2,1,0:T(8,128)(2,1)}, bf16[8,16,416]{2,1,0:T(8,128)(2,1)}, bf16[4,768,768]{2,1,0:T(8,128)(2,1)}, bf16[4,768,768]{2,1,0:T(8,128)(2,1)}) custom-call(s32[2]{0:T(128)} %pad_add_fusion.place_ref, bf16[8,16,416]{2,1,0:T(8,128)(2,1)} %get-tuple-element.37.flag_ref.flags_all, ...), custom_call_target="tpu_custom_call" | custom-call | flops 49999998976 | bytes 50000000 | tf_op jit(solution)/shard_map/experts/pallas_call | solution.py:670
  169.5 152.4 %tail.1 = (bf16[394,768]{1,0:T(8,128)(2,1)}, bf16[394,768]{1,0:T(8,128)(2,1)}, bf16[384,3072]{1,0:T(8,128)(2,1)}, f32[16,384]{1,0:T(8,128)}, bf16[8,384,768]{2,1...) custom-call(bf16[8,416,768]{2,1,0:T(8,128)(2,1)} %get-tuple-element.42.ba, ...), custom_call_target="tpu_custom_call" | custom-call | flops 16000000000 | bytes 50000000 | tf_op jit(solution)/shard_map/tail/pallas_call | solution.py:1245
  321.9 1.5 slice_reduce_fusion
  323.5 1.3 slice_bitcast_fusion
  324.8 2.3 slice.29
  327.1 0.0 copy-done
  327.1 2.0 slice.28
  329.1 4.6 %convert_element_type.12 = f32[8,384,768]{2,1,0:T(8,128)} convert(bf16[8,384,768]{2,1,0:T(8,128)(2,1)S(1)} %copy-done.1) | non-fusion elementwise | flops 2359296 | bytes 14155776 | tf_op jit(solution)/shard_map/convert_element_type | solution.py:1480
  333.7 0.0 slice-done
  333.7 4.4 %convert_element_type.13 = f32[8,768,384]{2,1,0:T(8,128)} convert(bf16[8,768,384]{2,1,0:T(8,128)(2,1)S(1)} %bitcast.12) | non-fusion elementwise | flops 2359296 | bytes 14155776 | tf_op jit(solution)/shard_map/convert_element_type | solution.py:1481
  338.1 0.8 copy.31
  338.9 0.8 copy.32
  (16 shorter events, 0.1 us)
Async XLA Ops:
  321.9 5.1 %copy-start = (bf16[384,3072]{1,0:T(8,128)(2,1)S(1)}, bf16[384,3072]{1,0:T(8,128)(2,1)}, u32[]{:S(2)}) copy-start(bf16[384,3072]{1,0:T(8,128)(2,1)} %get-tuple-element.60) | copy-start | bytes 7077892
  324.8 4.3 %copy-start.1 = (bf16[8,384,768]{2,1,0:T(8,128)(2,1)S(1)}, bf16[8,384,768]{2,1,0:T(8,128)(2,1)}, u32[]{:S(2)}) copy-start(bf16[8,384,768]{2,1,0:T(8,128)(2,1)} %get-tuple-element.61) | copy-start | bytes 14155780
  327.1 6.6 %slice-start = ((s8[4718592]{0:T(1024)(128)(4,1)}), s8[4194304]{0:T(1024)(128)(4,1)S(1)}, s32[]{:S(2)}) async-start(s8[4718592]{0:T(1024)(128)(4,1)} %bitcast.11), calls=%async_computation | async-start | bytes 8388608
  329.1 4.6 %slice-start.1 = ((s8[4718592]{0:T(1024)(128)(4,1)}), s8[524288]{0:T(1024)(128)(4,1)S(1)}, s32[]{:S(2)}) async-start(s8[4718592]{0:T(1024)(128)(4,1)} %bitcast.11), calls=%async_computation.1 | async-start | bytes 1048576
  333.7 4.4 %copy-start.3 = (bf16[394,768]{1,0:T(8,128)(2,1)S(1)}, bf16[394,768]{1,0:T(8,128)(2,1)}, u32[]{:S(2)}) copy-start(bf16[394,768]{1,0:T(8,128)(2,1)} %get-tuple-element.78) | copy-start | bytes 1815556
  333.7 5.2 %copy-start.2 = (bf16[394,768]{1,0:T(8,128)(2,1)S(1)}, bf16[394,768]{1,0:T(8,128)(2,1)}, u32[]{:S(2)}) copy-start(bf16[394,768]{1,0:T(8,128)(2,1)} %get-tuple-element.79) | copy-start | bytes 1815556

commit v3 on v2

--- a/solution.py
+++ b/solution.py
@@ -249,7 +249,7 @@
 
 def pad_images(source, target):
     value = source[...].astype(F32)
-    empty = jnp.zeros((PAD - SEQ, value.shape[1]), F32)
+    empty = jnp.zeros((PAD - SEQ, source.shape[1]), F32)
     for image in range(2):
         part = value[image * SEQ : (image + 1) * SEQ]
         target[pl.ds(image * PAD, PAD), :] = jnp.concatenate((part, empty), 0).astype(BF)
@@ -352,6 +352,7 @@
         _, target = expert_item(item)
         forwarded.append(links.start(target, target, place.beside))
 
+    forward_expert(0)
     for image in range(2):
         normed, prob, flag = front_image(
             image, experts, x_ref, small_ref, qkv_ref, out_ref, noise_ref, ids_ref, keep,
@@ -363,7 +364,8 @@
         twin_rows.append(links.start(sent_rows.at[at, :], rows_all.at[mine, at, :], place.twin))
         probs.append(prob)
         flags.append(flag)
-        forward_expert(image)
+        if image == 1:
+            forward_expert(1)
     prob_ref[...] = jnp.concatenate(probs, 1)
     sent_flags[...] = jnp.concatenate(flags, 1).astype(BF)
     flag_line.start(0, 0)
@@ -816,7 +818,7 @@
     )(moe, gates, cot, x, middle, sent, flags, prob, attended, packed, normed, small, qkv, out)
 
 
-ORDER = [[('x', 0), ('n', 3)], [('a', 0), ('x', 1), ('n', 4)], [], [('b', 0), ('n', 5), ('x', 2), ('y', 0), ('y', 1)], [('n', 6), ('a', 1)], [('x', 3), ('c', 0)], [('da', 1), ('x', 4)], [('x', 5), ('da', 0), ('n', 7), ('dl', 1), ('y', 2), ('x', 6)], [('dl', 0)], [('da', 3), ('db', 1), ('x', 7), ('n', 8), ('db', 0), ('n', 9), ('da', 2), ('dl', 3), ('y', 3), ('n', 10), ('b', 1), ('ds', 1), ('ds', 0), ('x', 8)], [('y', 4), ('c', 1), ('y', 5), ('x', 9), ('dl', 2), ('s', 0), ('db', 3), ('n', 11), ('y', 6), ('d1', 0), ('y', 7), ('ds', 3), ('s', 1), ('db', 2), ('x', 10), ('y', 8)], [('d2', 0), ('ds', 2), ('d1', 1), ('x', 11), ('dt', 3), ('s', 2), ('d1', 2), ('d2', 1), ('y', 9), ('dt', 0), ('y', 10), ('d2', 2), ('y', 11), ('s', 3), ('dt', 1), ('dt', 2)]]
+ORDER = [[('x', 0), ('a', 0), ('n', 3), ('n', 4)], [('x', 1)], [], [('x', 2), ('y', 0), ('x', 3), ('n', 5), ('b', 0), ('x', 4)], [('n', 6), ('a', 1)], [], [('x', 5), ('da', 1)], [('da', 0), ('y', 1), ('dl', 1), ('x', 6), ('b', 1), ('n', 7), ('n', 8)], [('da', 3), ('dl', 0), ('n', 9), ('x', 7)], [('db', 0), ('db', 1)], [('y', 2), ('x', 8), ('da', 2), ('ds', 0), ('y', 3), ('dl', 3), ('y', 4), ('s', 0), ('n', 10), ('c', 0), ('y', 5), ('x', 9), ('dl', 2), ('s', 1), ('y', 6), ('d1', 0), ('db', 3), ('ds', 1), ('n', 11), ('y', 7), ('c', 1), ('db', 2), ('x', 10), ('d2', 0), ('ds', 3), ('ds', 2), ('d1', 1), ('dt', 0), ('x', 11), ('y', 8), ('dt', 3), ('s', 2), ('d1', 2), ('y', 9)], [('d2', 1), ('y', 10), ('s', 3), ('d2', 2), ('y', 11), ('dt', 1), ('dt', 2)]]
 
 
 class LineScatter:
@@ -992,56 +994,65 @@
     share = depth // 2
     piece = share // 4
     stage = {}
+    early, late = width * 5 // 2, width * 2 // 3
+    spans = (
+        pl.ds(0, width), pl.ds(width, early - width), pl.ds(early, late), pl.ds(early + late, 4 * width - early - late),
+    )
+
+    def fill(k):
+        columns = pl.ds(spans[k].start - width, spans[k].size)
+        chunks[:, spans[k]] = contract_rows(normed_ref[...], stacked[:, columns]).astype(BF)
+        dense_core(k)
 
     def dense_core(k):
         stage["core", k] = []
         for owner in range(2):
-            source = chunks.at[k, pl.ds(pl.multiple_of(owner * depth + (1 - pair) * share, TALL), share), :]
-            stage["core", k].append(links.start(source, core_got.at[k, owner], place.twin))
+            source = chunks.at[pl.ds(pl.multiple_of(owner * depth + (1 - pair) * share, TALL), share), spans[k]]
+            stage["core", k].append(links.start(source, core_got.at[owner, :, spans[k]], place.twin))
 
     def core_sum(k, owner):
         at = pl.ds(pl.multiple_of(owner * depth + pair * share, TALL), share)
-        return chunks[k, at, :].astype(F32) + core_got[k, owner].astype(F32)
+        return chunks[at, spans[k]].astype(F32) + core_got[owner, :, spans[k]].astype(F32)
 
     def dense_across(k):
         for copy in stage["core", k]:
             copy.wait_recv()
-        across_sent[k] = core_sum(k, 1 - shard).astype(BF)
-        stage["across", k] = links.start(across_sent.at[k], across_got.at[k], place.across)
+        across_sent[:, spans[k]] = core_sum(k, 1 - shard).astype(BF)
+        stage["across", k] = links.start(across_sent.at[:, spans[k]], across_got.at[:, spans[k]], place.across)
 
     def around(offset):
         return (shard, place.head, lax.rem(tensor + offset, 4))
 
     def dense_line(k):
         stage["across", k].wait_recv()
-        line_sum[k] = (core_sum(k, shard) + across_got[k].astype(F32)).astype(BF)
+        line_sum[:, spans[k]] = (core_sum(k, shard) + across_got[:, spans[k]].astype(F32)).astype(BF)
         stage["line", k] = []
         for offset in (2, 1, 3):
             at = pl.ds(pl.multiple_of(lax.rem(tensor + offset, 4) * piece, TALL), piece)
-            stage["line", k].append(links.start(line_sum.at[k, at, :], line_got.at[k, offset - 1], around(offset)))
+            stage["line", k].append(links.start(line_sum.at[at, spans[k]], line_got.at[offset - 1, :, spans[k]], around(offset)))
 
     def dense_beside(k):
         for copy in stage["line", k]:
             copy.wait_recv()
         at = pl.ds(pl.multiple_of(tensor * piece, TALL), piece)
-        value = line_sum[k, at, :].astype(F32)
+        value = line_sum[at, spans[k]].astype(F32)
         for offset in range(3):
-            value = value + line_got[k, offset].astype(F32)
-        side_sum[k] = value.astype(BF)
-        stage["beside", k] = links.start(side_sum.at[k], side_got.at[k], place.beside)
+            value = value + line_got[offset, :, spans[k]].astype(F32)
+        side_sum[:, spans[k]] = value.astype(BF)
+        stage["beside", k] = links.start(side_sum.at[:, spans[k]], side_got.at[:, spans[k]], place.beside)
 
     def dense_spread(k):
         stage["beside", k].wait_recv()
-        line_final[k] = (side_sum[k].astype(F32) + side_got[k].astype(F32)).astype(BF)
+        line_final[:, spans[k]] = (side_sum[:, spans[k]].astype(F32) + side_got[:, spans[k]].astype(F32)).astype(BF)
         target = dense_ref.at[
-            pl.ds(pl.multiple_of(pair * share + tensor * piece, TALL), piece), pl.ds(k * width, width)
+            pl.ds(pl.multiple_of(pair * share + tensor * piece, TALL), piece), spans[k]
         ]
-        stage["keep", k] = pltpu.make_async_copy(line_final.at[k], target, local_sem.at[24 + k])
+        stage["keep", k] = pltpu.make_async_copy(line_final.at[:, spans[k]], target, local_sem.at[24 + k])
         stage["keep", k].start()
         if k < 3:
             dense_line_back.start(k, 0)
         else:
-            stage["spread", k] = [links.start(line_final.at[k], target, around(offset)) for offset in (2, 1, 3)]
+            stage["spread", k] = [links.start(line_final.at[:, spans[k]], target, around(offset)) for offset in (2, 1, 3)]
 
     def dense_hop(k, step):
         dense_line_back.wait(k, step)
@@ -1050,9 +1061,9 @@
     dense_line_back = LineGather(
         links, place,
         lambda slot, k: dense_ref.at[
-            pl.ds(pl.multiple_of(pair * share + slot * piece, TALL), piece), pl.ds(k * width, width)
+            pl.ds(pl.multiple_of(pair * share + slot * piece, TALL), piece), spans[k]
         ],
-        lambda k: line_final.at[k], 3,
+        lambda k: line_final.at[:, spans[k]], 3,
     )
 
     def dense_twin(k):
@@ -1062,7 +1073,7 @@
             for copy in stage["spread", k]:
                 copy.wait_recv()
         stage["keep", k].wait()
-        block = dense_ref.at[pl.ds(pl.multiple_of(pair * share, TALL), share), pl.ds(k * width, width)]
+        block = dense_ref.at[pl.ds(pl.multiple_of(pair * share, TALL), share), spans[k]]
         stage["twin", k] = links.start(block, block, place.twin)
 
     def small_core_stage():
@@ -1184,12 +1195,11 @@
     use_heads(0, 0)
     go(4)
     middle_of(1)
-    chunks[0] = contract_rows(attended_ref[...], projected[...]).astype(BF)
+    chunks[:, spans[0]] = contract_rows(attended_ref[...], projected[...]).astype(BF)
     dense_core(0)
     go(5)
     use_heads(0, 1)
-    chunks[1] = contract_rows(normed_ref[...], stacked[:, pl.ds(0, width)]).astype(BF)
-    dense_core(1)
+    fill(1)
     go(6)
     for part in range(2):
         total_line.send(part, 1)
@@ -1197,8 +1207,7 @@
     go(7)
     use_heads(1, 1)
     for k in (2, 3):
-        chunks[k] = contract_rows(normed_ref[...], stacked[:, pl.ds((k - 1) * width, width)]).astype(BF)
-        dense_core(k)
+        fill(k)
     go(8)
     for part in range(2):
         total_line.send(part, 2)
@@ -1267,15 +1276,15 @@
             pltpu.VMEM((rows, width), BF),
             pltpu.VMEM((rows, 3 * width), BF),
             pltpu.VMEM((24, PAD, PAD), BF),
-            pltpu.VMEM((4, width, width), BF),
-            pltpu.VMEM((4, 2, share, width), BF),
-            pltpu.VMEM((4, share, width), BF),
-            pltpu.VMEM((4, share, width), BF),
-            pltpu.VMEM((4, share, width), BF),
-            pltpu.VMEM((4, 3, piece, width), BF),
-            pltpu.VMEM((4, piece, width), BF),
-            pltpu.VMEM((4, piece, width), BF),
-            pltpu.VMEM((4, piece, width), BF),
+            pltpu.VMEM((width, 4 * width), BF),
+            pltpu.VMEM((2, share, 4 * width), BF),
+            pltpu.VMEM((share, 4 * width), BF),
+            pltpu.VMEM((share, 4 * width), BF),
+            pltpu.VMEM((share, 4 * width), BF),
+            pltpu.VMEM((3, piece, 4 * width), BF),
+            pltpu.VMEM((piece, 4 * width), BF),
+            pltpu.VMEM((piece, 4 * width), BF),
+            pltpu.VMEM((piece, 4 * width), BF),
         ]
         + [pltpu.VMEM((depth, hidden), BF), pltpu.VMEM((hidden, depth), BF)]
         + [pltpu.VMEM((count - 1, depth, hidden), BF), pltpu.VMEM((count - 1, hidden, depth), BF)]

time: 345 us -> 344 us (level)
  no operation moved by 1% of the time
where the time goes in v3:
time: 344 us; the launch traced here: 337 us
  Pallas kernels  310 us (90%)
  local copies, waits for them, and re-layouts  15.5 us (5%)
  other arithmetic  10.8 us (3%)
    pallas_call x1, Pallas kernels, tail(): pl.pallas_call(tail_kernel, out_shape=(shape((rows // PAD * SEQ, width),...  150 us
    pallas_call x1, Pallas kernels, head(): pl.pallas_call(head_kernel, out_shape=(shape((2, TALL, depth), BF), shape...  90.4 us
    pallas_call x1, Pallas kernels, expert_pass(): pl.pallas_call(expert_kernel, out_shape=(shape((blocks, length, width), B...  69.8 us

profile of v3, /device:TPU:17, one launch (start us, length us, event | category | flops | bytes accessed | tf_op | source)
XLA Modules:
  0.0 337.3 jit_solution(17727854773400703198)
XLA Ops:
  0.7 0.6 pad_add_fusion.place_ref
  1.2 0.8 reshape.40
  2.0 0.9 dynamic-update-slice
  2.9 0.9 dynamic-update-slice.1
  3.7 0.9 dynamic-update-slice.2
  4.6 0.9 dynamic-update-slice.3
  5.4 0.3 dynamic-update-slice.4
  5.7 1.3 pad_maximum_fusion.small_own
  7.0 0.7 reshape.41.ids_ref
  7.7 0.8 reshape.38
  8.5 0.7 reshape.39.noise_ref
  9.2 90.4 %head.1 = (bf16[2,16,384]{2,1,0:T(8,128)(2,1)}, bf16[768,2304]{1,0:T(8,128)(2,1)}, bf16[768,768]{1,0:T(8,128)(2,1)}, bf16[416,768]{1,0:T(8,128)(2,1)}, bf16[416,...) custom-call(bf16[394,768]{1,0:T(8,128)(2,1)} %tokens_own.1, ...), custom_call_target="tpu_custom_call" | custom-call | flops 8000000000 | bytes 30000000 | tf_op jit(solution)/shard_map/head/pallas_call | solution.py:424
  99.7 69.8 %experts.1 = (bf16[8,416,768]{2,1,0:T(8,128)(2,1)}, bf16[8,416,768]{2,1,0:T(8,128)(2,1)}, bf16[8,16,416]{2,1,0:T(8,128)(2,1)}, bf16[4,768,768]{2,1,0:T(8,128)(2,1)}, bf16[4,768,768]{2,1,0:T(8,128)(2,1)}) custom-call(s32[2]{0:T(128)} %pad_add_fusion.place_ref, bf16[8,16,416]{2,1,0:T(8,128)(2,1)} %get-tuple-element.37.flag_ref.flags_all, ...), custom_call_target="tpu_custom_call" | custom-call | flops 49999998976 | bytes 50000000 | tf_op jit(solution)/shard_map/experts/pallas_call | solution.py:672
  169.5 149.7 %tail.1 = (bf16[394,768]{1,0:T(8,128)(2,1)}, bf16[394,768]{1,0:T(8,128)(2,1)}, bf16[384,3072]{1,0:T(8,128)(2,1)}, f32[16,384]{1,0:T(8,128)}, bf16[8,384,768]{2,1...) custom-call(bf16[8,416,768]{2,1,0:T(8,128)(2,1)} %get-tuple-element.42.ba, ...), custom_call_target="tpu_custom_call" | custom-call | flops 16000000000 | bytes 50000000 | tf_op jit(solution)/shard_map/tail/pallas_call | solution.py:1254
  319.3 1.5 slice_reduce_fusion
  320.8 1.3 slice_bitcast_fusion
  322.1 2.3 slice.29
  324.4 0.0 copy-done
  324.4 2.0 slice.28
  326.4 4.6 %convert_element_type.12 = f32[8,384,768]{2,1,0:T(8,128)} convert(bf16[8,384,768]{2,1,0:T(8,128)(2,1)S(1)} %copy-done.1) | non-fusion elementwise | flops 2359296 | bytes 14155776 | tf_op jit(solution)/shard_map/convert_element_type | solution.py:1489
  331.0 0.0 slice-done
  331.0 4.4 %convert_element_type.13 = f32[8,768,384]{2,1,0:T(8,128)} convert(bf16[8,768,384]{2,1,0:T(8,128)(2,1)S(1)} %bitcast.12) | non-fusion elementwise | flops 2359296 | bytes 14155776 | tf_op jit(solution)/shard_map/convert_element_type | solution.py:1490
  335.4 0.8 copy.31
  336.2 0.8 copy.32
  (16 shorter events, 0.1 us)
Async XLA Ops:
  319.2 5.1 %copy-start = (bf16[384,3072]{1,0:T(8,128)(2,1)S(1)}, bf16[384,3072]{1,0:T(8,128)(2,1)}, u32[]{:S(2)}) copy-start(bf16[384,3072]{1,0:T(8,128)(2,1)} %get-tuple-element.60) | copy-start | bytes 7077892
  322.1 4.3 %copy-start.1 = (bf16[8,384,768]{2,1,0:T(8,128)(2,1)S(1)}, bf16[8,384,768]{2,1,0:T(8,128)(2,1)}, u32[]{:S(2)}) copy-start(bf16[8,384,768]{2,1,0:T(8,128)(2,1)} %get-tuple-element.61) | copy-start | bytes 14155780
  324.4 6.6 %slice-start = ((s8[4718592]{0:T(1024)(128)(4,1)}), s8[4194304]{0:T(1024)(128)(4,1)S(1)}, s32[]{:S(2)}) async-start(s8[4718592]{0:T(1024)(128)(4,1)} %bitcast.11), calls=%async_computation | async-start | bytes 8388608
  326.4 4.6 %slice-start.1 = ((s8[4718592]{0:T(1024)(128)(4,1)}), s8[524288]{0:T(1024)(128)(4,1)S(1)}, s32[]{:S(2)}) async-start(s8[4718592]{0:T(1024)(128)(4,1)} %bitcast.11), calls=%async_computation.1 | async-start | bytes 1048576
  331.0 4.4 %copy-start.3 = (bf16[394,768]{1,0:T(8,128)(2,1)S(1)}, bf16[394,768]{1,0:T(8,128)(2,1)}, u32[]{:S(2)}) copy-start(bf16[394,768]{1,0:T(8,128)(2,1)} %get-tuple-element.78) | copy-start | bytes 1815556
  331.0 5.2 %copy-start.2 = (bf16[394,768]{1,0:T(8,128)(2,1)S(1)}, bf16[394,768]{1,0:T(8,128)(2,1)}, u32[]{:S(2)}) copy-start(bf16[394,768]{1,0:T(8,128)(2,1)} %get-tuple-element.79) | copy-start | bytes 1815556
